TPU v7x, 32 devices: a whole 2x2x4 slice. The times are simulated.
32 devices in a mesh: ens: 1, tile: 32 (over z, y, x, core).
Axes of the slice: x: 2, y: 2, z: 4, core: 2. Of those that a mesh axis runs over, the one named last changes fastest.
Arguments:
- ocean_field: bfloat16 [131072, 128], P(('ens', 'tile')), may hold values from -6 to 6
- ocean_mask: int32 [131072], P('tile'), may hold values 0 or 1
- remap_weight: bfloat16 [8192, 128, 128], P('tile'), may hold values from -0.125 to 0.125
- source_tile: int32 [8192], P('tile'), may hold values from 0 to 31
- target_tile: int32 [8192], replicated, may hold values from 0 to 15
- dest_device: int32 [8192, 1], replicated, may hold values from 0 to 31, as said below
- atm_state: bfloat16 [65536, 128], P(('ens', 'tile')), may hold values from -6 to 6
- kappa: float32 [65536, 128], P('tile'), may hold values from 0.05 to 0.24
- mix: bfloat16 [128, 128], replicated, may hold values from -0.5 to 0.5
- cotangent: bfloat16 [65536, 128], P(('ens', 'tile')), may hold values from -6 to 6
Outputs:
- atm_next: bfloat16 [65536, 128], P(('ens', 'tile'))
- atm_grad: bfloat16 [65536, 128], P(('ens', 'tile'))
- ocean_grad: bfloat16 [131072, 128], P(('ens', 'tile'))
Inputs may be any that keep to these rules, and one draw needn't show every extreme that they name: `dest_device`: the 256 entries of owner device o name only devices o - 4 to o + 4, counted modulo the devices of tile; at most 64 of them name the same device, and in every owner exactly 64 name one device.
All inputs are finite; a program needn't handle non-finite values. No bound on the sum of `ocean_mask` on one device may be relied on, other than what follows from the above.
Results may differ from a plain program's by a relative error of at most 0.0053.
Values may be sent and summed in bfloat16 or wider, within the bound.
A program may use at most 192 MiB of HBM per device.

v0:
```python
import jax
import jax.numpy as jnp
from jax import lax
from jax.sharding import PartitionSpec as P

WIN = 4
CAP = 64


def passed_along(value, axis, steps):
    count = lax.axis_size(axis)
    pairs = [(source, (source + steps) % count) for source in range(count)]
    return lax.ppermute(value, axis, pairs)


def with_halo(array, sides, width):
    for axis, dim in sides:
        count, length = (lax.axis_size(axis), array.shape[dim])
        up = [(i, (i + 1) % count) for i in range(count)]
        down = [(j, i) for i, j in up]
        last = lax.slice_in_dim(array, length - width, length, axis=dim)
        leading = lax.slice_in_dim(array, 0, width, axis=dim)
        before = lax.ppermute(last, axis, up)
        after = lax.ppermute(leading, axis, down)
        array = jnp.concatenate([before, array, after], axis=dim)
    return array


def shards(
    ocean_field,
    ocean_mask,
    remap_weight,
    source_tile,
    target_tile,
    dest_device,
    atm_state,
    kappa,
    mix,
    cotangent,
):
    devices = lax.axis_size("tile")
    myself = lax.axis_index("tile")
    entry_count = remap_weight.shape[0]
    tile_cells = remap_weight.shape[1]
    channels = ocean_field.shape[1]
    ocn_count = ocean_field.shape[0] // tile_cells
    atm_count = atm_state.shape[0] // tile_cells
    span = 2 * WIN + 1
    slots = span * CAP
    keep = (ocean_mask == 1)[:, None]
    masked = jnp.where(keep, ocean_field, jnp.zeros_like(ocean_field))
    ocean_tiles = masked.reshape(ocn_count, tile_cells, channels)
    picked = ocean_tiles[source_tile]
    products = jnp.einsum(
        "eij,ejc->eic", remap_weight, picked, preferred_element_type=jnp.float32
    ).astype(jnp.bfloat16)
    dest_all = dest_device[:, 0].reshape(devices, entry_count)
    targets_all = target_tile.reshape(devices, entry_count)
    owner_ids = jnp.arange(devices, dtype=jnp.int32)[:, None]
    offset_all = (dest_all - owner_ids + WIN) % devices
    onehot_off = (
        offset_all[:, :, None] == jnp.arange(span, dtype=jnp.int32)[None, None, :]
    ).astype(jnp.int32)
    ranking_all = jnp.sum((jnp.cumsum(onehot_off, axis=1) - onehot_off) * onehot_off, axis=2)
    position_all = offset_all * CAP + ranking_all
    own_offset = lax.dynamic_index_in_dim(offset_all, myself, 0, keepdims=False)
    own_target = lax.dynamic_index_in_dim(targets_all, myself, 0, keepdims=False)
    slot_index = lax.dynamic_index_in_dim(position_all, myself, 0, keepdims=False)
    outgoing = jnp.zeros((slots, tile_cells, channels), jnp.bfloat16).at[slot_index].set(products)
    outgoing = outgoing.reshape(span, CAP, tile_cells, channels)
    arrived = []
    for offset in range(-WIN, WIN + 1):
        block = outgoing[offset + WIN]
        if offset == 0:
            arrived.append(block)
        else:
            arrived.append(passed_along(block, "tile", offset))
    received = jnp.stack(arrived, axis=0).reshape(slots, tile_cells, channels)
    arrives = dest_all == myself
    position = jnp.where(arrives, position_all, slots)
    slot_target = (
        jnp.full((slots + 1,), -1, jnp.int32)
        .at[position.reshape(-1)]
        .set(jnp.where(arrives, targets_all, -1).reshape(-1))[:slots]
    )
    onehot_target = (
        slot_target[None, :] == jnp.arange(atm_count, dtype=jnp.int32)[:, None]
    ).astype(jnp.bfloat16)
    imported = jnp.dot(
        onehot_target,
        received.reshape(slots, tile_cells * channels),
        preferred_element_type=jnp.float32,
    )
    forcing = atm_state.astype(jnp.float32) + imported.reshape(atm_count * tile_cells, channels)
    padded = with_halo(forcing, (("tile", 0),), 1)
    smooth = forcing + kappa * (padded[:-2] + padded[2:] - 2.0 * forcing)
    tanh_smooth = jnp.tanh(smooth)
    hval = tanh_smooth.astype(jnp.bfloat16)
    atm_next = jnp.dot(hval, mix, preferred_element_type=jnp.float32).astype(jnp.bfloat16)
    grad_tanh = jnp.dot(cotangent, mix.T, preferred_element_type=jnp.float32)
    grad_smooth = grad_tanh * (1.0 - tanh_smooth * tanh_smooth)
    weighted = kappa * grad_smooth
    padded_adj = with_halo(weighted, (("tile", 0),), 1)
    atm_grad = (grad_smooth + padded_adj[:-2] + padded_adj[2:] - 2.0 * weighted).astype(
        jnp.bfloat16
    )
    grad_blocks = atm_grad.reshape(atm_count, tile_cells, channels)
    nearby = []
    for offset in range(-WIN, WIN + 1):
        if offset == 0:
            nearby.append(grad_blocks)
        else:
            nearby.append(passed_along(grad_blocks, "tile", -offset))
    near_tiles = jnp.stack(nearby, axis=0).reshape(span * atm_count, tile_cells, channels)
    own_tiles = near_tiles[own_offset * atm_count + own_target]
    contrib = jnp.einsum(
        "eji,ejc->eic", remap_weight, own_tiles, preferred_element_type=jnp.float32
    )
    onehot_source = (
        source_tile[None, :] == jnp.arange(ocn_count, dtype=jnp.int32)[:, None]
    ).astype(jnp.float32)
    ocean_sum = jnp.dot(
        onehot_source,
        contrib.reshape(entry_count, tile_cells * channels),
        precision=lax.Precision.HIGHEST,
    )
    ocean_sum = ocean_sum.reshape(ocn_count * tile_cells, channels)
    ocean_grad = jnp.where(keep, ocean_sum, jnp.zeros_like(ocean_sum)).astype(jnp.bfloat16)
    return (atm_next, atm_grad, ocean_grad)


def solution(mesh):
    return jax.shard_map(
        shards,
        mesh=mesh,
        in_specs=(
            P(("ens", "tile"), None),
            P("tile"),
            P("tile", None, None),
            P("tile"),
            P(),
            P(),
            P(("ens", "tile"), None),
            P("tile", None),
            P(),
            P(("ens", "tile"), None),
        ),
        out_specs=(P(("ens", "tile"), None), P(("ens", "tile"), None), P(("ens", "tile"), None)),
        check_vma=False,
    )
```

profile of v0, /device:TPU:0, one launch (start us, length us, event | category | flops | bytes accessed | tf_op | source)
XLA Modules:
  0.0 593.0 jit_solution(6021999895334167795)
XLA Ops:
  5.8 18.1 %reduce-window.6 = s32[32,9,2,128]{3,1,2,0:T(8,128)S(1)} reduce-window(s32[32,9,2,128]{3,1,2,0:T(8,128)S(1)} %fusion.14, s32[]{:T(128)} %constant.28.clone.1), window={size=1x1x1x128 pad=0_0x0_0x0_0x127_0}, to_apply=%region_0.1 | reduce-window | flops 9363456 | bytes 589828 | tf_op jit(solution)/shard_map/reduce-window
  25.2 3.4 broadcast_select_fusion
  28.6 8.6 %gather_fusion = bf16[256,128,128]{2,1,0:T(8,128)(2,1)} fusion(bf16[32,128,128]{2,1,0:T(8,128)(2,1)S(1)} %bitcast.90, s32[1024]{0:T(1024)S(1)} %pad_clamp_fusion.1), kind=kCustom, calls=%fused_computation | custom fusion | bytes 16778240 | tf_op jit(solution)/shard_map/gather | solution.py:53
  37.2 11.6 %convert_bitcast_fusion = bf16[256,128,128]{1,2,0:T(8,128)(2,1)} fusion(bf16[256,128,128]{2,1,0:T(8,128)(2,1)} %gather_fusion, bf16[256,128,128]{2,1,0:T(8,128)(2,1)} %param.12), kind=kOutput, calls=%fused_computation.8 | convolution fusion | flops 1077936128 | bytes 25165824 | tf_op jit(solution)/shard_map/eij,ejc->eic/dot_general | solution.py:54
  48.8 12.0 %copy.18 = bf16[256,128,128]{2,1,0:T(8,128)(2,1)} copy(bf16[256,128,128]{1,2,0:T(8,128)(2,1)} %convert_bitcast_fusion) | data formatting | bytes 16777216 | tf_op jit(solution)/shard_map/convert_element_type | solution.py:56
  60.8 7.1 %broadcast_in_dim.50 = bf16[576,128,128]{2,1,0:T(8,128)(2,1)} broadcast(bf16[]{:T(256)} %constant.59.clone.1), dimensions={} | broadcast | bytes 18874370 | tf_op jit(solution)/shard_map/broadcast_in_dim | solution.py:69
  67.9 37.7 %scatter_fusion = bf16[576,128,128]{2,1,0:T(8,128)(2,1)} fusion(bf16[576,128,128]{2,1,0:T(8,128)(2,1)} %broadcast_in_dim.50, s32[256]{0:T(256)S(1)} %bitcast.108, bf16[256,128,128]{2,1,0:T(8,128)(2,1)} %copy.18), kind=kCustom, calls=%fused_computation.3 | custom fusion | bytes 25166848 | tf_op jit(solution)/shard_map/scatter | solution.py:69
  105.6 11.2 %fusion.29 = (bf16[64,128,128]{2,1,0:T(8,128)(2,1)S(1)}, bf16[64,128,128]{2,1,0:T(8,128)(2,1)}, bf16[64,128,128]{2,1,0:T(8,128)(2,1)}, bf16[64,128,128]{2,1,0:T(...) fusion(bf16[576,128,128]{2,1,0:T(8,128)(2,1)} %scatter_fusion), kind=kLoop, calls=%fused_computation.89 | loop fusion | bytes 33554432 | tf_op jit(solution)/shard_map/slice | solution.py:73
  116.8 6.9 %collective-permute-start.2 = (bf16[64,128,128]{2,1,0:T(8,128)(2,1)S(1)}, bf16[64,128,128]{2,1,0:T(8,128)(2,1)S(1)}, u32[]{:S(2)}, u32[]{:S(2)}) collective-permute-start(bf16[64,128,128]{2,1,0:T(8,128)(2,1)S(1)} %get-tuple-element.8), channel_id=1, source_target_pairs={{0,30},{1,31},{2,0},{3,1},{4,2},{5,3},{6,4},{7,5},{8,6},{9,7},{10,... | collective-permute-start | bytes 6291464 | tf_op jit(solution)/shard_map/ppermute | solution.py:13
  123.7 5.3 collective-permute-start.3
  129.4 72.8 %collective-permute-done.2 = bf16[64,128,128]{2,1,0:T(8,128)(2,1)S(1)} collective-permute-done((bf16[64,128,128]{2,1,0:T(8,128)(2,1)S(1)}, bf16[64,128,128]{2,1,0:T(8,128)(2,1)S(1)}, u32[]{:S(2)}, u32[]{:S(2)}) %collective-permute-start.2) | collective-permute-done | bytes 2097184 | tf_op jit(solution)/shard_map/ppermute | solution.py:13
  203.6 30.4 %scatter_custom_fusion = s32[577]{0:T(1024)S(1)} fusion(s32[8192]{0:T(1024)S(1)} %bitcast.107, s32[8192]{0:T(1024)S(1)} %broadcast_select_fusion.1, s32[]{:T(128)} %constant.22.clone.1), kind=kCustom, calls=%fused_computation.84 | custom fusion | bytes 2312 | tf_op jit(solution)/shard_map/scatter | solution.py:84
  234.1 125.9 %collective-permute-done = bf16[64,128,128]{2,1,0:T(8,128)(2,1)} collective-permute-done((bf16[64,128,128]{2,1,0:T(8,128)(2,1)}, bf16[64,128,128]{2,1,0:T(8,128)(2,1)}, u32[]{:S(2)}, u32[]{:S(2)}) %collective-permute-start) | collective-permute-done | bytes 2097184 | tf_op jit(solution)/shard_map/ppermute | solution.py:13
  360.0 3.2 bitcast_dynamic-update-slice_fusion.7
  363.2 7.7 %collective-permute-start.7 = (bf16[64,128,128]{2,1,0:T(8,128)(2,1)S(1)}, bf16[64,128,128]{2,1,0:T(8,128)(2,1)S(1)}, u32[]{:S(2)}, u32[]{:S(2)}) collective-permute-start(bf16[64,128,128]{2,1,0:T(8,128)(2,1)S(1)} %get-tuple-element.3), channel_id=1, source_target_pairs={{0,4},{1,5},{2,6},{3,7},{4,8},{5,9},{6,10},{7,11},{8,12},{9,13},{1... | collective-permute-start | bytes 6291464 | tf_op jit(solution)/shard_map/ppermute | solution.py:13
  375.5 3.2 bitcast_dynamic-update-slice_fusion.4
  378.7 3.2 fusion.3
  381.9 3.2 bitcast_dynamic-update-slice_fusion.3
  385.1 3.2 bitcast_dynamic-update-slice_fusion.2
  388.3 16.3 %collective-permute-done.6 = bf16[64,128,128]{2,1,0:T(8,128)(2,1)S(1)} collective-permute-done((bf16[64,128,128]{2,1,0:T(8,128)(2,1)}, bf16[64,128,128]{2,1,0:T(8,128)(2,1)S(1)}, u32[]{:S(2)}, u32[]{:S(2)}) %collective-permute-start.6) | collective-permute-done | bytes 2097184 | tf_op jit(solution)/shard_map/ppermute | solution.py:13
  406.0 11.0 %collective-permute-done.7 = bf16[64,128,128]{2,1,0:T(8,128)(2,1)S(1)} collective-permute-done((bf16[64,128,128]{2,1,0:T(8,128)(2,1)S(1)}, bf16[64,128,128]{2,1,0:T(8,128)(2,1)S(1)}, u32[]{:S(2)}, u32[]{:S(2)}) %collective-permute-start.7) | collective-permute-done | bytes 2097184 | tf_op jit(solution)/shard_map/ppermute | solution.py:13
  418.5 18.6 %fusion = f32[16,16384]{1,0:T(8,128)S(1)} fusion(bf16[72,8,128,128]{3,2,1,0:T(8,128)(2,1)} %bitcast.42, s32[576]{0:T(1024)S(1)} %bitcast.105), kind=kOutput, calls=%fused_computation.4 | convolution fusion | flops 301999104 | bytes 19925248 | tf_op jit(solution)/shard_map/dot_general | solution.py:89
  437.4 18.9 %collective-permute-start.8 = (f32[1,128]{1,0:T(1,128)S(1)}, f32[1,128]{1,0:T(1,128)S(1)}, u32[]{:S(2)}, u32[]{:S(2)}) collective-permute-start(f32[1,128]{1,0:T(1,128)S(1)} %get-tuple-element.13), channel_id=1, source_target_pairs={{0,1},{1,2},{2,3},{3,4},{4,5},{5,6},{6,7},{7,8},{8,9},{9,10},{10,1... | collective-permute-start | bytes 1544 | tf_op jit(solution)/shard_map/ppermute | solution.py:23
  461.2 3.6 collective-permute-start.11
  470.0 3.8 collective-permute-start.19
  475.1 37.4 %collective-permute-done.12 = bf16[16,128,128]{2,1,0:T(8,128)(2,1)S(1)} collective-permute-done((bf16[16,128,128]{2,1,0:T(8,128)(2,1)S(1)}, bf16[16,128,128]{2,1,0:T(8,128)(2,1)S(1)}, u32[]{:S(2)}, u32[]{:S(2)}) %collective-permute-start.12) | collective-permute-done | bytes 524320 | tf_op jit(solution)/shard_map/ppermute | solution.py:13
  515.1 6.9 %collective-permute-start.16 = (bf16[16,128,128]{2,1,0:T(8,128)(2,1)S(1)}, bf16[16,128,128]{2,1,0:T(8,128)(2,1)S(1)}, u32[]{:S(2)}, u32[]{:S(2)}) collective-permute-start(bf16[16,128,128]{2,1,0:T(8,128)(2,1)S(1)} %bitcast.99), channel_id=1, source_target_pairs={{0,31},{1,0},{2,1},{3,2},{4,3},{5,4},{6,5},{7,6},{8,7},{9,8},{10,9... | collective-permute-start | bytes 1572872 | tf_op jit(solution)/shard_map/ppermute | solution.py:13
  526.5 5.6 collective-permute-done.16
  535.6 11.0 %gather_fusion.1 = bf16[256,128,128]{2,1,0:T(8,128)(2,1)} fusion(bf16[144,128,128]{2,1,0:T(8,128)(2,1)} %bitcast.27, s32[1024]{0:T(1024)S(1)} %pad_clamp_fusion), kind=kCustom, calls=%fused_computation.1 | custom fusion | bytes 16778240 | tf_op jit(solution)/shard_map/gather | solution.py:115
  546.5 14.4 %convolution_bitcast_fusion = f32[256,128,128]{1,2,0:T(8,128)} fusion(bf16[256,128,128]{2,1,0:T(8,128)(2,1)} %gather_fusion.1, bf16[256,128,128]{2,1,0:T(8,128)(2,1)} %param.12), kind=kOutput, calls=%fused_computation.7 | convolution fusion | flops 1073741824 | bytes 33554432 | tf_op jit(solution)/shard_map/eji,ejc->eic/dot_general | solution.py:116
  560.9 17.8 %copy.20 = f32[256,128,128]{0,2,1:T(8,128)} copy(f32[256,128,128]{1,2,0:T(8,128)} %convolution_bitcast_fusion) | data formatting | bytes 33554432 | tf_op jit(solution)/shard_map/eji,ejc->eic/dot_general | solution.py:116
  578.7 10.9 %fusion.22 = bf16[32,16384]{1,0:T(8,128)(2,1)S(1)} fusion(f32[256,16384]{0,1:T(8,128)} %bitcast.91, s32[256]{0:T(256)S(1)} %copy-done.9), kind=kOutput, calls=%fused_computation.74 | convolution fusion | flops 1610620928 | bytes 17826816 | tf_op jit(solution)/shard_map/dot_general | solution.py:122
  (96 shorter events, 41.4 us)
Async XLA Ops:
  0.6 456.9 %copy-start = (bf16[2048,128]{1,0:T(8,128)(2,1)S(1)}, bf16[2048,128]{1,0:T(8,128)(2,1)}, u32[]{:S(2)}) copy-start(bf16[2048,128]{1,0:T(8,128)(2,1)} %param.19) | copy-start | bytes 1572868
  105.6 23.5 %copy-start.6 = (s32[8192,1]{0,1:T(1,128)S(1)}, s32[8192,1]{0,1:T(1,128)}, u32[]{:S(2)}) copy-start(s32[8192,1]{0,1:T(1,128)} %param.15) | copy-start | bytes 98308
  105.6 98.0 %copy-start.7 = (s32[8192]{0:T(1024)S(1)}, s32[8192]{0:T(1024)}, u32[]{:S(2)}) copy-start(s32[8192]{0:T(1024)} %param.14) | copy-start | bytes 98308
  116.8 85.5 %collective-permute-start.2 = (bf16[64,128,128]{2,1,0:T(8,128)(2,1)S(1)}, bf16[64,128,128]{2,1,0:T(8,128)(2,1)S(1)}, u32[]{:S(2)}, u32[]{:S(2)}) collective-permute-start(bf16[64,128,128]{2,1,0:T(8,128)(2,1)S(1)} %get-tuple-element.8), channel_id=1, source_target_pairs={{0,30},{1,31},{2,0},{3,1},{4,2},{5,3},{6,4},{7,5},{8,6},{9,7},{10,... | collective-permute-start | bytes 6291464 | tf_op jit(solution)/shard_map/ppermute | solution.py:13
  123.7 258.2 %collective-permute-start.4 = (bf16[64,128,128]{2,1,0:T(8,128)(2,1)}, bf16[64,128,128]{2,1,0:T(8,128)(2,1)}, u32[]{:S(2)}, u32[]{:S(2)}) collective-permute-start(bf16[64,128,128]{2,1,0:T(8,128)(2,1)} %get-tuple-element.6), channel_id=1, source_target_pairs={{0,1},{1,2},{2,3},{3,4},{4,5},{5,6},{6,7},{7,8},{8,9},{9,10},{10,1... | collective-permute-start | bytes 6291464 | tf_op jit(solution)/shard_map/ppermute | solution.py:13
  123.7 251.8 %collective-permute-start.3 = (bf16[64,128,128]{2,1,0:T(8,128)(2,1)}, bf16[64,128,128]{2,1,0:T(8,128)(2,1)}, u32[]{:S(2)}, u32[]{:S(2)}) collective-permute-start(bf16[64,128,128]{2,1,0:T(8,128)(2,1)} %get-tuple-element.7), channel_id=1, source_target_pairs={{0,31},{1,0},{2,1},{3,2},{4,3},{5,4},{6,5},{7,6},{8,7},{9,8},{10,9... | collective-permute-start | bytes 6291464 | tf_op jit(solution)/shard_map/ppermute | solution.py:13
  129.0 234.1 %collective-permute-start.1 = (bf16[64,128,128]{2,1,0:T(8,128)(2,1)}, bf16[64,128,128]{2,1,0:T(8,128)(2,1)}, u32[]{:S(2)}, u32[]{:S(2)}) collective-permute-start(bf16[64,128,128]{2,1,0:T(8,128)(2,1)} %get-tuple-element.9), channel_id=1, source_target_pairs={{0,29},{1,30},{2,31},{3,0},{4,1},{5,2},{6,3},{7,4},{8,5},{9,6},{10... | collective-permute-start | bytes 6291464 | tf_op jit(solution)/shard_map/ppermute | solution.py:13
  129.0 231.0 %collective-permute-start = (bf16[64,128,128]{2,1,0:T(8,128)(2,1)}, bf16[64,128,128]{2,1,0:T(8,128)(2,1)}, u32[]{:S(2)}, u32[]{:S(2)}) collective-permute-start(bf16[64,128,128]{2,1,0:T(8,128)(2,1)} %get-tuple-element.10), channel_id=1, source_target_pairs={{0,28},{1,29},{2,30},{3,31},{4,0},{5,1},{6,2},{7,3},{8,4},{9,5},{1... | collective-permute-start | bytes 6291464 | tf_op jit(solution)/shard_map/ppermute | solution.py:13
  202.3 1.4 copy-start.2
  203.6 181.5 %collective-permute-start.5 = (bf16[64,128,128]{2,1,0:T(8,128)(2,1)}, bf16[64,128,128]{2,1,0:T(8,128)(2,1)}, u32[]{:S(2)}, u32[]{:S(2)}) collective-permute-start(bf16[64,128,128]{2,1,0:T(8,128)(2,1)} %get-tuple-element.5), channel_id=1, source_target_pairs={{0,2},{1,3},{2,4},{3,5},{4,6},{5,7},{6,8},{7,9},{8,10},{9,11},{10,... | collective-permute-start | bytes 6291464 | tf_op jit(solution)/shard_map/ppermute | solution.py:13
  234.1 139.9 %copy-start.3 = (bf16[64,128,128]{2,1,0:T(8,128)(2,1)S(1)}, bf16[64,128,128]{2,1,0:T(8,128)(2,1)}, u32[]{:S(2)}) copy-start(bf16[64,128,128]{2,1,0:T(8,128)(2,1)} %copy-done.2) | copy-start | bytes 6291460
  360.0 44.6 %collective-permute-start.6 = (bf16[64,128,128]{2,1,0:T(8,128)(2,1)}, bf16[64,128,128]{2,1,0:T(8,128)(2,1)S(1)}, u32[]{:S(2)}, u32[]{:S(2)}) collective-permute-start(bf16[64,128,128]{2,1,0:T(8,128)(2,1)} %get-tuple-element.4), channel_id=1, source_target_pairs={{0,3},{1,4},{2,5},{3,6},{4,7},{5,8},{6,9},{7,10},{8,11},{9,12},{10... | collective-permute-start | bytes 6291464 | tf_op jit(solution)/shard_map/ppermute | solution.py:13
  363.2 53.9 %collective-permute-start.7 = (bf16[64,128,128]{2,1,0:T(8,128)(2,1)S(1)}, bf16[64,128,128]{2,1,0:T(8,128)(2,1)S(1)}, u32[]{:S(2)}, u32[]{:S(2)}) collective-permute-start(bf16[64,128,128]{2,1,0:T(8,128)(2,1)S(1)} %get-tuple-element.3), channel_id=1, source_target_pairs={{0,4},{1,5},{2,6},{3,7},{4,8},{5,9},{6,10},{7,11},{8,12},{9,13},{1... | collective-permute-start | bytes 6291464 | tf_op jit(solution)/shard_map/ppermute | solution.py:13
  418.5 18.7 %copy-start.5 = (bf16[2048,128]{1,0:T(8,128)(2,1)S(1)}, bf16[2048,128]{1,0:T(8,128)(2,1)}, u32[]{:S(2)}) copy-start(bf16[2048,128]{1,0:T(8,128)(2,1)} %param.16) | copy-start | bytes 1572868
  418.5 39.1 %copy-start.8 = (bf16[128,128]{1,0:T(8,128)(2,1)S(1)}, bf16[128,128]{1,0:T(8,128)(2,1)}, u32[]{:S(2)}) copy-start(bf16[128,128]{1,0:T(8,128)(2,1)} %param.18) | copy-start | bytes 98308
  437.2 31.4 %copy-start.4 = (f32[2048,128]{1,0:T(8,128)S(1)}, f32[2048,128]{1,0:T(8,128)}, u32[]{:S(2)}) copy-start(f32[2048,128]{1,0:T(8,128)} %param.17) | copy-start | bytes 3145732
  437.4 19.7 %collective-permute-start.8 = (f32[1,128]{1,0:T(1,128)S(1)}, f32[1,128]{1,0:T(1,128)S(1)}, u32[]{:S(2)}, u32[]{:S(2)}) collective-permute-start(f32[1,128]{1,0:T(1,128)S(1)} %get-tuple-element.13), channel_id=1, source_target_pairs={{0,1},{1,2},{2,3},{3,4},{4,5},{5,6},{6,7},{7,8},{8,9},{9,10},{10,1... | collective-permute-start | bytes 1544 | tf_op jit(solution)/shard_map/ppermute | solution.py:23
  456.3 1.3 collective-permute-start.9
  459.4 6.6 %collective-permute-start.10 = (f32[1,128]{1,0:T(1,128)S(1)}, f32[1,128]{1,0:T(1,128)S(1)}, u32[]{:S(2)}, u32[]{:S(2)}) collective-permute-start(f32[1,128]{1,0:T(1,128)S(1)} %get-tuple-element.11), channel_id=1, source_target_pairs={{0,1},{1,2},{2,3},{3,4},{4,5},{5,6},{6,7},{7,8},{8,9},{9,10},{10,1... | collective-permute-start | bytes 1544 | tf_op jit(solution)/shard_map/ppermute | solution.py:23
  461.2 4.9 collective-permute-start.11
  466.4 80.1 %copy-start.1 = (bf16[2048,128]{1,0:T(8,128)(2,1)}, bf16[2048,128]{1,0:T(8,128)(2,1)S(1)}, u32[]{:S(2)}) copy-start(bf16[2048,128]{1,0:T(8,128)(2,1)S(1)} %fusion.6) | copy-start | bytes 1572868
  466.4 46.0 %collective-permute-start.12 = (bf16[16,128,128]{2,1,0:T(8,128)(2,1)S(1)}, bf16[16,128,128]{2,1,0:T(8,128)(2,1)S(1)}, u32[]{:S(2)}, u32[]{:S(2)}) collective-permute-start(bf16[16,128,128]{2,1,0:T(8,128)(2,1)S(1)} %bitcast.92), channel_id=1, source_target_pairs={{0,4},{1,5},{2,6},{3,7},{4,8},{5,9},{6,10},{7,11},{8,12},{9,13},{1... | collective-permute-start | bytes 1572872 | tf_op jit(solution)/shard_map/ppermute | solution.py:13
  466.5 48.6 %collective-permute-start.14 = (bf16[16,128,128]{2,1,0:T(8,128)(2,1)S(1)}, bf16[16,128,128]{2,1,0:T(8,128)(2,1)S(1)}, u32[]{:S(2)}, u32[]{:S(2)}) collective-permute-start(bf16[16,128,128]{2,1,0:T(8,128)(2,1)S(1)} %bitcast.93), channel_id=1, source_target_pairs={{0,2},{1,3},{2,4},{3,5},{4,6},{5,7},{6,8},{7,9},{8,10},{9,11},{10,... | collective-permute-start | bytes 1572872 | tf_op jit(solution)/shard_map/ppermute | solution.py:13
  466.8 46.5 %collective-permute-start.13 = (bf16[16,128,128]{2,1,0:T(8,128)(2,1)S(1)}, bf16[16,128,128]{2,1,0:T(8,128)(2,1)S(1)}, u32[]{:S(2)}, u32[]{:S(2)}) collective-permute-start(bf16[16,128,128]{2,1,0:T(8,128)(2,1)S(1)} %bitcast.94), channel_id=1, source_target_pairs={{0,3},{1,4},{2,5},{3,6},{4,7},{5,8},{6,9},{7,10},{8,11},{9,12},{10... | collective-permute-start | bytes 1572872 | tf_op jit(solution)/shard_map/ppermute | solution.py:13
  470.0 64.7 %collective-permute-start.19 = (bf16[16,128,128]{2,1,0:T(8,128)(2,1)S(1)}, bf16[16,128,128]{2,1,0:T(8,128)(2,1)S(1)}, u32[]{:S(2)}, u32[]{:S(2)}) collective-permute-start(bf16[16,128,128]{2,1,0:T(8,128)(2,1)S(1)} %bitcast.95), channel_id=1, source_target_pairs={{0,28},{1,29},{2,30},{3,31},{4,0},{5,1},{6,2},{7,3},{8,4},{9,5},{1... | collective-permute-start | bytes 1572872 | tf_op jit(solution)/shard_map/ppermute | solution.py:13
  473.8 60.1 %collective-permute-start.18 = (bf16[16,128,128]{2,1,0:T(8,128)(2,1)S(1)}, bf16[16,128,128]{2,1,0:T(8,128)(2,1)S(1)}, u32[]{:S(2)}, u32[]{:S(2)}) collective-permute-start(bf16[16,128,128]{2,1,0:T(8,128)(2,1)S(1)} %bitcast.96), channel_id=1, source_target_pairs={{0,29},{1,30},{2,31},{3,0},{4,1},{5,2},{6,3},{7,4},{8,5},{9,6},{10... | collective-permute-start | bytes 1572872 | tf_op jit(solution)/shard_map/ppermute | solution.py:13
  512.5 12.4 %collective-permute-start.15 = (bf16[16,128,128]{2,1,0:T(8,128)(2,1)S(1)}, bf16[16,128,128]{2,1,0:T(8,128)(2,1)S(1)}, u32[]{:S(2)}, u32[]{:S(2)}) collective-permute-start(bf16[16,128,128]{2,1,0:T(8,128)(2,1)S(1)} %bitcast.97), channel_id=1, source_target_pairs={{0,1},{1,2},{2,3},{3,4},{4,5},{5,6},{6,7},{7,8},{8,9},{9,10},{10,1... | collective-permute-start | bytes 1572872 | tf_op jit(solution)/shard_map/ppermute | solution.py:13
  513.3 19.7 %collective-permute-start.17 = (bf16[16,128,128]{2,1,0:T(8,128)(2,1)S(1)}, bf16[16,128,128]{2,1,0:T(8,128)(2,1)S(1)}, u32[]{:S(2)}, u32[]{:S(2)}) collective-permute-start(bf16[16,128,128]{2,1,0:T(8,128)(2,1)S(1)} %bitcast.98), channel_id=1, source_target_pairs={{0,30},{1,31},{2,0},{3,1},{4,2},{5,3},{6,4},{7,5},{8,6},{9,7},{10,... | collective-permute-start | bytes 1572872 | tf_op jit(solution)/shard_map/ppermute | solution.py:13
  515.1 17.1 %collective-permute-start.16 = (bf16[16,128,128]{2,1,0:T(8,128)(2,1)S(1)}, bf16[16,128,128]{2,1,0:T(8,128)(2,1)S(1)}, u32[]{:S(2)}, u32[]{:S(2)}) collective-permute-start(bf16[16,128,128]{2,1,0:T(8,128)(2,1)S(1)} %bitcast.99), channel_id=1, source_target_pairs={{0,31},{1,0},{2,1},{3,2},{4,3},{5,4},{6,5},{7,6},{8,7},{9,8},{10,9... | collective-permute-start | bytes 1572872 | tf_op jit(solution)/shard_map/ppermute | solution.py:13
  560.9 17.8 %copy-start.9 = (s32[256]{0:T(256)S(1)}, s32[256]{0:T(256)}, u32[]{:S(2)}) copy-start(s32[256]{0:T(256)} %param.13) | copy-start | bytes 3076
where the time goes:
time: 602 us; the launch traced here: 593 us
  waiting for transfers between devices  274 us (46%)
  local copies, waits for them, and re-layouts  171 us (28%)
  starting transfers between devices  59.3 us (10%)
  matrix products  58.5 us (10%)
  other arithmetic  29.3 us (5%)
    ppermute x16, waiting for transfers between devices, passed_along(): return lax.ppermute(value, axis, pairs)  271 us
    scatter x1, local copies, waits for them, and re-layouts, shards(): jnp.zeros((slots, tile_cells, channels), jnp.bfloat16).at[slot_index]  37.7 us
    ppermute x16, starting transfers between devices, passed_along(): return lax.ppermute(value, axis, pairs)  35 us
    unnamed x40, local copies, waits for them, and re-layouts  30.8 us
    scatter x1, local copies, waits for them, and re-layouts, shards(): slot_target = jnp.full((slots + 1,), -1, jnp.int32).at[position.reshape(-...  30.4 us
    ppermute x2, starting transfers between devices, with_halo(): before = lax.ppermute(last, axis, up)  20.7 us
    dot_general x1, matrix products, shards(): jnp.dot(onehot_target, received.reshape(slots, tile_cells * channels), pr...  18.6 us
    another operation x3, other arithmetic  18.4 us
  transfers between devices with their start and end apart: 20, of which 11 were waited for; matrix products, arithmetic and copies ran while one was open for 10% of the time, Pallas kernels for 0%

commit v1 on v0

v1 whole, which is shorter than its diff:
```python
import functools

import jax
import jax.numpy as jnp
from jax import lax
from jax.experimental import pallas as pl
from jax.experimental.pallas import tpu as pltpu
from jax.sharding import PartitionSpec as P

WIN = 4
SPAN = 2 * WIN + 1
HALO = 8
STEPS = 16
VMEM_BYTES = 56 * 1024 * 1024
OFFSETS = [o for d in range(1, WIN + 1) for o in (d, -d)]
FAR_FIRST = OFFSETS[::-1]


def diagonal(row, size):
    eye = lax.broadcasted_iota(jnp.int32, (size, size), 0) == lax.broadcasted_iota(
        jnp.int32, (size, size), 1
    )
    return jnp.where(eye, jnp.broadcast_to(row, (size, size)), 0).astype(jnp.bfloat16)


def forward_kernel(per, src_ref, slot_ref, ocean_ref, mask_ref, w_ref, out_ref, acc, xm):
    step = pl.program_id(0)
    tile = w_ref.shape[1]

    @pl.when(step == 0)
    def _():
        def clear(i, carry):
            acc[i] = jnp.zeros(acc.shape[1:], acc.dtype)
            return carry

        lax.fori_loop(0, acc.shape[0], clear, 0)

        def mask_tile(i, carry):
            keep = jnp.where(mask_ref[pl.ds(i, 1), :] == 1, 1.0, 0.0)
            xm[i] = jnp.dot(
                diagonal(keep, tile), ocean_ref[i], preferred_element_type=jnp.float32
            ).astype(jnp.bfloat16)
            return carry

        lax.fori_loop(0, xm.shape[0], mask_tile, 0, unroll=4)

    for k in range(per):
        e = step * per + k
        product = jnp.dot(w_ref[k], xm[src_ref[e]], preferred_element_type=jnp.float32)
        acc[slot_ref[e]] += product

    @pl.when(step == pl.num_programs(0) - 1)
    def _():
        def narrow(i, carry):
            out_ref[i] = acc[i].astype(out_ref.dtype)
            return carry

        lax.fori_loop(0, acc.shape[0], narrow, 0, unroll=4)


def middle_kernel(
    devices, tile, part, atm_ref, kappa_ref, mix_ref, cot_ref,
    near, grad_ref, hval_ref,
    recv, fpad, wpad, gs, gt, lo, hi, lo2, hi2, own,
    psend, precv, hsend, hrecv, gsend, grecv, local_sem,
):
    me = lax.axis_index("tile")
    rows = atm_ref.shape[0]
    tiles = rows // tile

    def at(offset):
        return {"tile": lax.rem(me + offset + devices, devices)}

    def copy_to(src, dst, ssem, rsem, offset):
        return pltpu.make_async_remote_copy(
            src_ref=src, dst_ref=dst, send_sem=ssem, recv_sem=rsem,
            device_id=at(offset), device_id_type=pl.DeviceIdType.MESH,
        )

    barrier = pltpu.get_barrier_semaphore()
    for o in OFFSETS:
        pl.semaphore_signal(
            barrier, inc=1, device_id=at(o), device_id_type=pl.DeviceIdType.MESH
        )
    pl.semaphore_wait(barrier, len(OFFSETS))

    parts = {
        o: copy_to(part.at[o + WIN], recv.at[o + WIN], psend.at[o + WIN], precv.at[o + WIN], o)
        for o in OFFSETS
    }
    for o in FAR_FIRST:
        parts[o].start()
    mine = pltpu.make_async_copy(part.at[WIN], recv.at[WIN], local_sem.at[0])
    mine.start()

    def adjoint_mix(i, carry):
        at_rows = pl.ds(pl.multiple_of(i * tile, tile), tile)
        gt[at_rows, :] = lax.dot_general(
            cot_ref[at_rows, :], mix_ref[...], (((1,), (1,)), ((), ())),
            preferred_element_type=jnp.float32,
        )
        return carry

    lax.fori_loop(0, tiles, adjoint_mix, 0, unroll=2)
    mine.wait()

    def add_parts(slots, first):
        def body(i, carry):
            at_rows = pl.ds(pl.multiple_of(i * tile, tile), tile)
            pad_rows = pl.ds(pl.multiple_of(i * tile + HALO, HALO), tile)
            if first:
                total = atm_ref[at_rows, :].astype(jnp.float32)
            else:
                total = fpad[pad_rows, :]
            for slot in slots:
                total = total + recv[slot, at_rows, :].astype(jnp.float32)
            fpad[pad_rows, :] = total
            return carry

        lax.fori_loop(0, tiles, body, 0)

    add_parts([WIN], True)
    for d in range(1, WIN + 1):
        parts[d].wait_recv()
        parts[-d].wait_recv()
        add_parts([WIN + d, WIN - d], False)

    def edges(pad, low, high, k):
        up = copy_to(pad.at[pl.ds(rows, HALO), :], low, hsend.at[k], hrecv.at[k], 1)
        down = copy_to(pad.at[pl.ds(HALO, HALO), :], high, hsend.at[k + 1], hrecv.at[k + 1], -1)
        return up, down

    def window(pad, i):
        w = pad[pl.ds(pl.multiple_of(i * tile, tile), tile + 2 * HALO), :]
        return w[HALO - 1 : HALO - 1 + tile], w[HALO : HALO + tile], w[HALO + 1 : HALO + 1 + tile]

    fwd_edges = edges(fpad, lo, hi, 0)
    for c in fwd_edges:
        c.start()

    def primal(i, carry):
        at_rows = pl.ds(pl.multiple_of(i * tile, tile), tile)
        before, x, after = window(fpad, i)
        kappa = kappa_ref[at_rows, :]
        th = jnp.tanh(x + kappa * (before + after - 2.0 * x))
        hval_ref[at_rows, :] = th.astype(jnp.bfloat16)
        g = gt[at_rows, :] * (1.0 - th * th)
        gs[at_rows, :] = g
        wpad[pl.ds(pl.multiple_of(i * tile + HALO, HALO), tile), :] = kappa * g
        return carry

    lax.fori_loop(1, tiles - 1, primal, 0)
    for c in fwd_edges:
        c.wait()
    fpad[0:HALO, :] = lo[...]
    fpad[rows + HALO : rows + 2 * HALO, :] = hi[...]
    lax.fori_loop(0, 2, lambda j, c: primal(j * (tiles - 1), c), 0)

    adj_edges = edges(wpad, lo2, hi2, 2)
    for c in adj_edges:
        c.start()

    def adjoint(i, carry):
        at_rows = pl.ds(pl.multiple_of(i * tile, tile), tile)
        before, x, after = window(wpad, i)
        grad = gs[at_rows, :] + before + after - 2.0 * x
        grad_ref[at_rows, :] = grad.astype(jnp.bfloat16)
        own[at_rows, :] = grad.T.astype(jnp.bfloat16)
        return carry

    lax.fori_loop(1, tiles - 1, adjoint, 0)
    pieces = [(tile, rows - 2 * tile), (0, tile), (rows - tile, tile)]

    def grads(p, o):
        cut = pl.ds(pieces[p][0], pieces[p][1])
        slot = WIN - o
        return copy_to(
            own.at[cut, :], near.at[slot, cut, :], gsend.at[p, slot], grecv.at[p, slot], o
        )

    sends = [grads(0, o) for o in FAR_FIRST]
    for c in sends:
        c.start()
    for c in adj_edges:
        c.wait()
    wpad[0:HALO, :] = lo2[...]
    wpad[rows + HALO : rows + 2 * HALO, :] = hi2[...]
    lax.fori_loop(0, 2, lambda j, c: adjoint(j * (tiles - 1), c), 0)
    late = [grads(p, o) for p in (1, 2) for o in FAR_FIRST]
    for c in late:
        c.start()
    keep = pltpu.make_async_copy(own, near.at[WIN], local_sem.at[1])
    keep.start()
    keep.wait()
    for c in sends + late:
        c.wait()
    for o in OFFSETS:
        parts[o].wait_send()


def adjoint_kernel(
    per, src_ref, slot_ref, near_ref, mask_ref, mix_ref, w_ref, hval_ref, grad_ref,
    next_ref, grad_out_ref, ocean_ref, acc,
):
    step = pl.program_id(0)

    @pl.when(step == 0)
    def _():
        def clear(i, carry):
            acc[i] = jnp.zeros(acc.shape[1:], acc.dtype)
            return carry

        lax.fori_loop(0, acc.shape[0], clear, 0)

    next_ref[...] = jnp.dot(
        hval_ref[...], mix_ref[...], preferred_element_type=jnp.float32
    ).astype(jnp.bfloat16)
    grad_out_ref[...] = grad_ref[...]
    for k in range(per):
        e = step * per + k
        product = jnp.dot(near_ref[slot_ref[e]], w_ref[k], preferred_element_type=jnp.float32)
        acc[src_ref[e]] += product

    @pl.when(step == pl.num_programs(0) - 1)
    def _():
        def finish(i, carry):
            total = jnp.where(mask_ref[pl.ds(i, 1), :] == 1, acc[i], 0.0)
            ocean_ref[i] = total.T.astype(jnp.bfloat16)
            return carry

        lax.fori_loop(0, acc.shape[0], finish, 0, unroll=2)


def whole(shape):
    return pl.BlockSpec(shape, lambda i, *_: (0,) * len(shape))


def shards(
    ocean_field, ocean_mask, remap_weight, source_tile, target_tile, dest_device,
    atm_state, kappa, mix, cotangent,
):
    devices = lax.axis_size("tile")
    me = lax.axis_index("tile")
    entries, tile, _ = remap_weight.shape
    channels = ocean_field.shape[1]
    ocn = ocean_field.shape[0] // tile
    rows = atm_state.shape[0]
    atm = rows // tile
    slots = SPAN * atm
    per = entries // STEPS
    dest = lax.dynamic_slice_in_dim(dest_device.reshape(-1), me * entries, entries)
    target = lax.dynamic_slice_in_dim(target_tile, me * entries, entries)
    slot = lax.rem(dest - me + WIN + devices, devices) * atm + target
    mask = ocean_mask.reshape(ocn, tile)
    params = functools.partial(pltpu.CompilerParams, vmem_limit_bytes=VMEM_BYTES)

    part = pl.pallas_call(
        functools.partial(forward_kernel, per),
        out_shape=jax.ShapeDtypeStruct((slots, tile, channels), jnp.bfloat16),
        grid_spec=pltpu.PrefetchScalarGridSpec(
            num_scalar_prefetch=2,
            grid=(STEPS,),
            in_specs=[
                whole((ocn, tile, channels)),
                whole((ocn, tile)),
                pl.BlockSpec((per, tile, tile), lambda i, *_: (i, 0, 0)),
            ],
            out_specs=whole((slots, tile, channels)),
            scratch_shapes=[
                pltpu.VMEM((slots, tile, channels), jnp.float32),
                pltpu.VMEM((ocn, tile, channels), jnp.bfloat16),
            ],
        ),
        compiler_params=params(),
        name="remap_forward",
    )(source_tile, slot, ocean_field.reshape(ocn, tile, channels), mask, remap_weight)

    vmem = pl.BlockSpec(memory_space=pltpu.VMEM)
    hbm = pl.BlockSpec(memory_space=pl.ANY)
    f32 = lambda *shape: pltpu.VMEM(shape, jnp.float32)
    near, grad, hval = pl.pallas_call(
        functools.partial(middle_kernel, devices, tile),
        out_shape=(
            jax.ShapeDtypeStruct((SPAN, rows, channels), jnp.bfloat16),
            jax.ShapeDtypeStruct((rows, channels), jnp.bfloat16),
            jax.ShapeDtypeStruct((rows, channels), jnp.bfloat16),
        ),
        in_specs=[hbm, vmem, vmem, vmem, vmem],
        out_specs=(hbm, vmem, vmem),
        scratch_shapes=[
            pltpu.VMEM((SPAN, rows, channels), jnp.bfloat16),
            f32(rows + 2 * HALO, channels),
            f32(rows + 2 * HALO, channels),
            f32(rows, channels),
            f32(rows, channels),
            f32(HALO, channels),
            f32(HALO, channels),
            f32(HALO, channels),
            f32(HALO, channels),
            pltpu.VMEM((rows, channels), jnp.bfloat16),
            pltpu.SemaphoreType.DMA((SPAN,)),
            pltpu.SemaphoreType.DMA((SPAN,)),
            pltpu.SemaphoreType.DMA((4,)),
            pltpu.SemaphoreType.DMA((4,)),
            pltpu.SemaphoreType.DMA((3, SPAN)),
            pltpu.SemaphoreType.DMA((3, SPAN)),
            pltpu.SemaphoreType.DMA((2,)),
        ],
        compiler_params=params(collective_id=0, has_side_effects=True),
        name="exchange_and_step",
    )(part.reshape(SPAN, rows, channels), atm_state, kappa, mix, cotangent)

    cut = pl.BlockSpec((rows // STEPS, channels), lambda i, *_: (i, 0))
    atm_next, atm_grad, ocean_grad = pl.pallas_call(
        functools.partial(adjoint_kernel, per),
        out_shape=(
            jax.ShapeDtypeStruct((rows, channels), jnp.bfloat16),
            jax.ShapeDtypeStruct((rows, channels), jnp.bfloat16),
            jax.ShapeDtypeStruct((ocn, tile, channels), jnp.bfloat16),
        ),
        grid_spec=pltpu.PrefetchScalarGridSpec(
            num_scalar_prefetch=2,
            grid=(STEPS,),
            in_specs=[
                whole((slots, tile, channels)),
                whole((ocn, tile)),
                whole((channels, channels)),
                pl.BlockSpec((per, tile, tile), lambda i, *_: (i, 0, 0)),
                cut,
                cut,
            ],
            out_specs=(cut, cut, whole((ocn, tile, channels))),
            scratch_shapes=[pltpu.VMEM((ocn, channels, tile), jnp.float32)],
        ),
        compiler_params=params(),
        name="remap_adjoint",
    )(
        source_tile, slot, near.reshape(slots, tile, channels), mask, mix, remap_weight,
        hval, grad,
    )
    return atm_next, atm_grad, ocean_grad.reshape(ocn * tile, channels)


def solution(mesh):
    both = P(("ens", "tile"), None)
    return jax.shard_map(
        shards,
        mesh=mesh,
        in_specs=(
            both, P("tile"), P("tile", None, None), P("tile"), P(), P(),
            both, P("tile", None), P(), both,
        ),
        out_specs=(both, both, both),
        check_vma=False,
    )
```

time: 602 us -> 167 us (0.28); the launches traced: 593 us -> 166 us
  waiting for transfers between devices: 274 us -> 0 us
  local copies, waits for them, and re-layouts: 171 us -> 0 us
  Pallas kernels: 0 us -> 163 us
  starting transfers between devices: 59.3 us -> 0 us
  matrix products: 58.5 us -> 0 us
  other arithmetic: 29.3 us -> 2.02 us
    ppermute x20 -> x0, waiting for transfers between devices: 274 us -> none  [the longest x16 271 us: passed_along(): return lax.ppermute(value, axis, pairs)]
    pallas_call x0 -> x3, Pallas kernels: none -> 163 us  [the longest x1 129 us: shards(): pl.pallas_call(functools.partial(middle_kernel, devices, tile), out_shape...]
    scatter x2 -> x0, local copies, waits for them, and re-layouts: 68.2 us -> none  [the longest x1 37.7 us: shards(): jnp.zeros((slots, tile_cells, channels), jnp.bfloat16).at[slot_index]]
    ppermute x20 -> x0, starting transfers between devices: 59.3 us -> none  [the longest x16 35 us: passed_along(): return lax.ppermute(value, axis, pairs)]
    dot_general x6 -> x0, matrix products: 58.5 us -> none  [the longest x1 18.6 us: shards(): jnp.dot(onehot_target, received.reshape(slots, tile_cells * channels), pr...]
    unnamed x40 -> x0, local copies, waits for them, and re-layouts: 30.8 us -> none
    gather x2 -> x0, local copies, waits for them, and re-layouts: 19.6 us -> none  [the longest x1 11 us: shards(): own_tiles = near_tiles[own_offset * atm_count + own_target]]
    another operation x3 -> x0, other arithmetic: 18.4 us -> none
  transfers between devices with their start and end apart: 20 -> 0, of which waited for: 11 -> 0; matrix products, arithmetic and copies ran while one was open for 10% -> 0% of each run, Pallas kernels for 0% -> 0%
where the time goes in v1:
time: 167 us; the launch traced here: 166 us
  Pallas kernels  163 us (98%)
  other arithmetic  2.02 us (1%)
    pallas_call x1, Pallas kernels, shards(): pl.pallas_call(functools.partial(middle_kernel, devices, tile), out_shape...  129 us
    pallas_call x1, Pallas kernels, shards(): pl.pallas_call(functools.partial(forward_kernel, per), out_shape=jax.Shap...  17.5 us
    pallas_call x1, Pallas kernels, shards(): pl.pallas_call(functools.partial(adjoint_kernel, per), out_shape=(jax.Sha...  17.3 us

profile of v1, /device:TPU:0, one launch (start us, length us, event | category | flops | bytes accessed | tf_op | source)
XLA Modules:
  0.0 166.1 jit_solution(16164038465348807661)
XLA Ops:
  0.6 0.7 subtract_add_fusion
  1.3 1.3 fusion.2.slot_ref
  2.7 17.5 %remap_forward.1 = bf16[144,128,128]{2,1,0:T(8,128)(2,1)} custom-call(s32[256]{0:T(256)} %src_ref.3, s32[256]{0:T(256)} %fusion.2.slot_ref, bf16[32,128,128]{2,1,0:T(8,128)(2,1)} %bitcast.8, s32[32,128]{1,0:T(8,128)} %bitcast.9, bf16[256,128,128]{2,1,0:T(8,128)(2,1)} %w_ref.3), custom_call_target="tpu_custom_call" | custom-call | tf_op jit(solution)/shard_map/remap_forward/pallas_call | solution.py:257
  20.2 128.7 %exchange_and_step.1 = (bf16[9,2048,128]{2,1,0:T(8,128)(2,1)}, bf16[2048,128]{1,0:T(8,128)(2,1)}, bf16[2048,128]{1,0:T(8,128)(2,1)}) custom-call(bf16[9,2048,128]{2,1,0:T(8,128)(2,1)} %bitcast.6, bf16[2048,128]{1,0:T(8,128)(2,1)} %atm_ref.1, f32[2048,128]{1,0:T(8,128)} %kappa_ref.1, bf16[128,128]{1,0:T(8,128)(2,1)} %mix_ref.3, bf16[2048,128]{1,0:T(8,128)(2,1)} %cot_ref.1), custom_call_target="tpu_custom_call" | custom-call | tf_op jit(solution)/shard_map/exchange_and_step/pallas_call | solution.py:281
  148.8 17.3 %remap_adjoint.1 = (bf16[2048,128]{1,0:T(8,128)(2,1)}, bf16[2048,128]{1,0:T(8,128)(2,1)}, bf16[32,128,128]{2,1,0:T(8,128)(2,1)}) custom-call(s32[256]{0:T(256)} %src_ref.3, s32[256]{0:T(256)} %fusion.2.slot_ref, bf16[144,128,128]{2,1,0:T(8,128)(2,1)} %bitcast.7, s32[32,128]{1,0:T(8,128)} %bitcast.10, bf16[128,128]{1,0:T(8,128)(2,1)} %mix_ref.3, ...), custom_call_target="tpu_custom_call" | custom-call | tf_op jit(solution)/shard_map/remap_adjoint/pallas_call | solution.py:314

commit v2 on v1

--- a/solution.py
+++ b/solution.py
@@ -12,8 +12,6 @@
 HALO = 8
 STEPS = 16
 VMEM_BYTES = 56 * 1024 * 1024
-OFFSETS = [o for d in range(1, WIN + 1) for o in (d, -d)]
-FAR_FIRST = OFFSETS[::-1]
 
 
 def diagonal(row, size):
@@ -61,37 +59,67 @@
 def middle_kernel(
     devices, tile, part, atm_ref, kappa_ref, mix_ref, cot_ref,
     near, grad_ref, hval_ref,
-    recv, fpad, wpad, gs, gt, lo, hi, lo2, hi2, own,
-    psend, precv, hsend, hrecv, gsend, grecv, local_sem,
+    even, odd, recv, fpad, wpad, gs, gt, lo, hi, lo2, hi2, own,
+    local_sem, osend, orecv, psend, precv, hsend, hrecv, gsend, grecv, xsend, xrecv,
 ):
     me = lax.axis_index("tile")
+    core = lax.rem(me, 2)
+    partner = me + 1 - 2 * core
     rows = atm_ref.shape[0]
     tiles = rows // tile
+    far, alone = 4 - 4 * core, 4 * core
 
     def at(offset):
-        return {"tile": lax.rem(me + offset + devices, devices)}
-
-    def copy_to(src, dst, ssem, rsem, offset):
+        return lax.rem(me + offset + devices, devices)
+
+    def copy_to(src, dst, ssem, rsem, device):
         return pltpu.make_async_remote_copy(
             src_ref=src, dst_ref=dst, send_sem=ssem, recv_sem=rsem,
-            device_id=at(offset), device_id_type=pl.DeviceIdType.MESH,
+            device_id={"tile": device}, device_id_type=pl.DeviceIdType.MESH,
         )
 
+    loads = [
+        pltpu.make_async_copy(part.at[2 * m], even.at[m], local_sem.at[m]) for m in range(5)
+    ]
+    for c in loads:
+        c.start()
+
     barrier = pltpu.get_barrier_semaphore()
-    for o in OFFSETS:
+    for o in (1, -1, 2, -2, 4, -4):
         pl.semaphore_signal(
-            barrier, inc=1, device_id=at(o), device_id_type=pl.DeviceIdType.MESH
+            barrier, inc=1, device_id={"tile": at(o)}, device_id_type=pl.DeviceIdType.MESH
         )
-    pl.semaphore_wait(barrier, len(OFFSETS))
-
-    parts = {
-        o: copy_to(part.at[o + WIN], recv.at[o + WIN], psend.at[o + WIN], precv.at[o + WIN], o)
-        for o in OFFSETS
-    }
-    for o in FAR_FIRST:
-        parts[o].start()
-    mine = pltpu.make_async_copy(part.at[WIN], recv.at[WIN], local_sem.at[0])
-    mine.start()
+    pl.semaphore_wait(barrier, 6)
+
+    def swap(j):
+        return copy_to(part.at[2 * j + 1], odd.at[j], osend.at[j], orecv.at[j], partner)
+
+    def ship(m):
+        return copy_to(even.at[m], recv.at[m], psend.at[m], precv.at[m], at(2 * m - 4))
+
+    for j in (3 * core, 1 - core, 3 - core, 2 - core):
+        swap(j).start()
+    for c in loads:
+        c.wait()
+    ship(alone).start()
+
+    def combine(m):
+        j = m - 1 + core
+        swap(j).wait_recv()
+
+        def body(i, carry):
+            at_rows = pl.ds(pl.multiple_of(i * tile, tile), tile)
+            total = even[m, at_rows, :].astype(jnp.float32)
+            total = total + odd[j, at_rows, :].astype(jnp.float32)
+            even[m, at_rows, :] = total.astype(jnp.bfloat16)
+            return carry
+
+        lax.fori_loop(0, tiles, body, 0, unroll=2)
+
+    for m in (far, 1, 3):
+        combine(m)
+        ship(m).start()
+    swap(1 + core).wait_recv()
 
     def adjoint_mix(i, carry):
         at_rows = pl.ds(pl.multiple_of(i * tile, tile), tile)
@@ -99,35 +127,34 @@
             cot_ref[at_rows, :], mix_ref[...], (((1,), (1,)), ((), ())),
             preferred_element_type=jnp.float32,
         )
+        total = atm_ref[at_rows, :].astype(jnp.float32)
+        total = total + even[2, at_rows, :].astype(jnp.float32)
+        total = total + odd[1 + core, at_rows, :].astype(jnp.float32)
+        fpad[pl.ds(pl.multiple_of(i * tile + HALO, HALO), tile), :] = total
         return carry
 
     lax.fori_loop(0, tiles, adjoint_mix, 0, unroll=2)
-    mine.wait()
-
-    def add_parts(slots, first):
+
+    def add_parts(slots):
         def body(i, carry):
             at_rows = pl.ds(pl.multiple_of(i * tile, tile), tile)
             pad_rows = pl.ds(pl.multiple_of(i * tile + HALO, HALO), tile)
-            if first:
-                total = atm_ref[at_rows, :].astype(jnp.float32)
-            else:
-                total = fpad[pad_rows, :]
+            total = fpad[pad_rows, :]
             for slot in slots:
                 total = total + recv[slot, at_rows, :].astype(jnp.float32)
             fpad[pad_rows, :] = total
             return carry
 
-        lax.fori_loop(0, tiles, body, 0)
-
-    add_parts([WIN], True)
-    for d in range(1, WIN + 1):
-        parts[d].wait_recv()
-        parts[-d].wait_recv()
-        add_parts([WIN + d, WIN - d], False)
+        lax.fori_loop(0, tiles, body, 0, unroll=2)
+
+    for pair in ((1, 3), (0, 4)):
+        for m in pair:
+            ship(m).wait_recv()
+        add_parts(pair)
 
     def edges(pad, low, high, k):
-        up = copy_to(pad.at[pl.ds(rows, HALO), :], low, hsend.at[k], hrecv.at[k], 1)
-        down = copy_to(pad.at[pl.ds(HALO, HALO), :], high, hsend.at[k + 1], hrecv.at[k + 1], -1)
+        up = copy_to(pad.at[pl.ds(rows, HALO), :], low, hsend.at[k], hrecv.at[k], at(1))
+        down = copy_to(pad.at[pl.ds(HALO, HALO), :], high, hsend.at[k + 1], hrecv.at[k + 1], at(-1))
         return up, down
 
     def window(pad, i):
@@ -168,34 +195,61 @@
         own[at_rows, :] = grad.T.astype(jnp.bfloat16)
         return carry
 
+    pieces = [(tile, rows - 2 * tile), (0, tile), (rows - tile, tile)]
+
+    def grads(p, m):
+        cut = pl.ds(pieces[p][0], pieces[p][1])
+        return copy_to(
+            own.at[cut, :], near.at[2 * m, cut, :], gsend.at[p, m], grecv.at[p, m], at(4 - 2 * m)
+        )
+
+    def hand(p, m, src):
+        cut = pl.ds(pieces[p][0], pieces[p][1])
+        j = m - 1 + core
+        return copy_to(
+            src, near.at[2 * j + 1, cut, :], xsend.at[p, j], xrecv.at[p, j], partner
+        )
+
+    def own_cut(p):
+        return own.at[pl.ds(pieces[p][0], pieces[p][1]), :]
+
+    def near_cut(p, m):
+        return near.at[2 * m, pl.ds(pieces[p][0], pieces[p][1]), :]
+
     lax.fori_loop(1, tiles - 1, adjoint, 0)
-    pieces = [(tile, rows - 2 * tile), (0, tile), (rows - tile, tile)]
-
-    def grads(p, o):
-        cut = pl.ds(pieces[p][0], pieces[p][1])
-        slot = WIN - o
-        return copy_to(
-            own.at[cut, :], near.at[slot, cut, :], gsend.at[p, slot], grecv.at[p, slot], o
-        )
-
-    sends = [grads(0, o) for o in FAR_FIRST]
-    for c in sends:
-        c.start()
+    order = (0, 4, 1, 3)
+    for m in order:
+        grads(0, m).start()
+    hand(0, 2, own_cut(0)).start()
     for c in adj_edges:
         c.wait()
     wpad[0:HALO, :] = lo2[...]
     wpad[rows + HALO : rows + 2 * HALO, :] = hi2[...]
     lax.fori_loop(0, 2, lambda j, c: adjoint(j * (tiles - 1), c), 0)
-    late = [grads(p, o) for p in (1, 2) for o in FAR_FIRST]
-    for c in late:
-        c.start()
-    keep = pltpu.make_async_copy(own, near.at[WIN], local_sem.at[1])
+    for p in (1, 2):
+        for m in order:
+            grads(p, m).start()
+        hand(p, 2, own_cut(p)).start()
+    keep = pltpu.make_async_copy(own, near.at[2 * 2], local_sem.at[5])
     keep.start()
+    for m in (1, 3, far):
+        for p in range(3):
+            grads(p, m).wait_recv()
+            hand(p, m, near_cut(p, m)).start()
+    for p in range(3):
+        grads(p, alone).wait_recv()
     keep.wait()
-    for c in sends + late:
-        c.wait()
-    for o in OFFSETS:
-        parts[o].wait_send()
+    for p in range(3):
+        for j in range(4):
+            out = hand(p, j + 1 - core, own_cut(p))
+            out.wait_send()
+            out.wait_recv()
+        for m in order:
+            grads(p, m).wait_send()
+    for j in range(4):
+        swap(j).wait_send()
+    for m in order:
+        ship(m).wait_send()
 
 
 def adjoint_kernel(
@@ -288,7 +342,9 @@
         in_specs=[hbm, vmem, vmem, vmem, vmem],
         out_specs=(hbm, vmem, vmem),
         scratch_shapes=[
-            pltpu.VMEM((SPAN, rows, channels), jnp.bfloat16),
+            pltpu.VMEM((5, rows, channels), jnp.bfloat16),
+            pltpu.VMEM((4, rows, channels), jnp.bfloat16),
+            pltpu.VMEM((5, rows, channels), jnp.bfloat16),
             f32(rows + 2 * HALO, channels),
             f32(rows + 2 * HALO, channels),
             f32(rows, channels),
@@ -298,13 +354,17 @@
             f32(HALO, channels),
             f32(HALO, channels),
             pltpu.VMEM((rows, channels), jnp.bfloat16),
-            pltpu.SemaphoreType.DMA((SPAN,)),
-            pltpu.SemaphoreType.DMA((SPAN,)),
+            pltpu.SemaphoreType.DMA((6,)),
             pltpu.SemaphoreType.DMA((4,)),
             pltpu.SemaphoreType.DMA((4,)),
-            pltpu.SemaphoreType.DMA((3, SPAN)),
-            pltpu.SemaphoreType.DMA((3, SPAN)),
-            pltpu.SemaphoreType.DMA((2,)),
+            pltpu.SemaphoreType.DMA((5,)),
+            pltpu.SemaphoreType.DMA((5,)),
+            pltpu.SemaphoreType.DMA((4,)),
+            pltpu.SemaphoreType.DMA((4,)),
+            pltpu.SemaphoreType.DMA((3, 5)),
+            pltpu.SemaphoreType.DMA((3, 5)),
+            pltpu.SemaphoreType.DMA((3, 4)),
+            pltpu.SemaphoreType.DMA((3, 4)),
         ],
         compiler_params=params(collective_id=0, has_side_effects=True),
         name="exchange_and_step",

time: 167 us -> 122 us (0.73)
  Pallas kernels: 163 us -> 118 us
    pallas_call x1, Pallas kernels: 129 us -> 83.6 us  [shards(): pl.pallas_call(functools.partial(middle_kernel, devices, tile), out_shape...]
where the time goes in v2:
time: 122 us; the launch traced here: 121 us
  Pallas kernels  118 us (97%)
  other arithmetic  2.02 us (2%)
    pallas_call x1, Pallas kernels, shards(): pl.pallas_call(functools.partial(middle_kernel, devices, tile), out_shape...  83.6 us
    pallas_call x1, Pallas kernels, shards(): pl.pallas_call(functools.partial(forward_kernel, per), out_shape=jax.Shap...  17.5 us
    pallas_call x1, Pallas kernels, shards(): pl.pallas_call(functools.partial(adjoint_kernel, per), out_shape=(jax.Sha...  17.3 us

profile of v2, /device:TPU:0, one launch (start us, length us, event | category | flops | bytes accessed | tf_op | source)
XLA Modules:
  0.0 121.1 jit_solution(14511767356968992018)
XLA Ops:
  0.6 0.7 subtract_add_fusion
  1.3 1.3 %fusion.2.slot_ref = s32[256]{0:T(256)} fusion(s32[256]{0:T(256)S(1)} %bitcast.11, s32[8192]{0:T(1024)} %param.14, s32[]{:T(128)S(6)} %select_n.4), kind=kLoop, calls=%fused_computation.4 | loop fusion | flops 2048 | bytes 3076 | tf_op jit(solution)/shard_map/add | solution.py:307
  2.7 17.5 %remap_forward.1 = bf16[144,128,128]{2,1,0:T(8,128)(2,1)} custom-call(s32[256]{0:T(256)} %src_ref.3, s32[256]{0:T(256)} %fusion.2.slot_ref, bf16[32,128,128]{2,1,0:T(8,128)(2,1)} %bitcast.8, s32[32,128]{1,0:T(8,128)} %bitcast.9, bf16[256,128,128]{2,1,0:T(8,128)(2,1)} %w_ref.3), custom_call_target="tpu_custom_call" | custom-call | tf_op jit(solution)/shard_map/remap_forward/pallas_call | solution.py:311
  20.2 83.6 %exchange_and_step.1 = (bf16[9,2048,128]{2,1,0:T(8,128)(2,1)}, bf16[2048,128]{1,0:T(8,128)(2,1)}, bf16[2048,128]{1,0:T(8,128)(2,1)}) custom-call(bf16[9,2048,128]{2,1,0:T(8,128)(2,1)} %bitcast.6, bf16[2048,128]{1,0:T(8,128)(2,1)} %atm_ref.1, f32[2048,128]{1,0:T(8,128)} %kappa_ref.1, bf16[128,128]{1,0:T(8,128)(2,1)} %mix_ref.3, bf16[2048,128]{1,0:T(8,128)(2,1)} %cot_ref.1), custom_call_target="tpu_custom_call" | custom-call | tf_op jit(solution)/shard_map/exchange_and_step/pallas_call | solution.py:335
  103.8 17.3 %remap_adjoint.1 = (bf16[2048,128]{1,0:T(8,128)(2,1)}, bf16[2048,128]{1,0:T(8,128)(2,1)}, bf16[32,128,128]{2,1,0:T(8,128)(2,1)}) custom-call(s32[256]{0:T(256)} %src_ref.3, s32[256]{0:T(256)} %fusion.2.slot_ref, bf16[144,128,128]{2,1,0:T(8,128)(2,1)} %bitcast.7, s32[32,128]{1,0:T(8,128)} %bitcast.10, bf16[128,128]{1,0:T(8,128)(2,1)} %mix_ref.3, ...), custom_call_target="tpu_custom_call" | custom-call | tf_op jit(solution)/shard_map/remap_adjoint/pallas_call | solution.py:374

commit v3 on v2

--- a/solution.py
+++ b/solution.py
@@ -59,15 +59,18 @@
 def middle_kernel(
     devices, tile, part, atm_ref, kappa_ref, mix_ref, cot_ref,
     near, grad_ref, hval_ref,
-    even, odd, recv, fpad, wpad, gs, gt, lo, hi, lo2, hi2, own,
-    local_sem, osend, orecv, psend, precv, hsend, hrecv, gsend, grecv, xsend, xrecv,
+    even, odd, recv, relayed, fpad, wpad, gs, gt, lo, hi, lo2, hi2, own,
+    local_sem, osend, orecv, psend, precv, hsend, hrecv, gsend, grecv, xsend, xrecv, rsem,
 ):
     me = lax.axis_index("tile")
     core = lax.rem(me, 2)
     partner = me + 1 - 2 * core
     rows = atm_ref.shape[0]
     tiles = rows // tile
-    far, alone = 4 - 4 * core, 4 * core
+    side = lax.rem(me // 2, 2)
+    across = lax.rem(me + 2 - 4 * side + devices, devices)
+    far = 4 - 4 * core
+    direct, passed, joined, plain = 3 - 2 * side, 1 + 2 * side, 4 - 4 * side, 4 * side
 
     def at(offset):
         return lax.rem(me + offset + devices, devices)
@@ -97,11 +100,10 @@
     def ship(m):
         return copy_to(even.at[m], recv.at[m], psend.at[m], precv.at[m], at(2 * m - 4))
 
-    for j in (3 * core, 1 - core, 3 - core, 2 - core):
+    for j in (passed - core, 3 * core, direct - core, 2 - core):
         swap(j).start()
     for c in loads:
         c.wait()
-    ship(alone).start()
 
     def combine(m):
         j = m - 1 + core
@@ -116,9 +118,13 @@
 
         lax.fori_loop(0, tiles, body, 0, unroll=2)
 
-    for m in (far, 1, 3):
-        combine(m)
-        ship(m).start()
+    add_on = copy_to(even.at[passed], relayed, rsem.at[0], rsem.at[1], across)
+    combine(passed)
+    add_on.start()
+    combine(far)
+    ship(plain).start()
+    combine(direct)
+    ship(direct).start()
     swap(1 + core).wait_recv()
 
     def adjoint_mix(i, carry):
@@ -147,10 +153,23 @@
 
         lax.fori_loop(0, tiles, body, 0, unroll=2)
 
-    for pair in ((1, 3), (0, 4)):
-        for m in pair:
-            ship(m).wait_recv()
-        add_parts(pair)
+    add_on.wait_recv()
+
+    def join(i, carry):
+        at_rows = pl.ds(pl.multiple_of(i * tile, tile), tile)
+        total = even[joined, at_rows, :].astype(jnp.float32)
+        total = total + relayed[at_rows, :].astype(jnp.float32)
+        even[joined, at_rows, :] = total.astype(jnp.bfloat16)
+        return carry
+
+    lax.fori_loop(0, tiles, join, 0, unroll=2)
+    ship(joined).start()
+    ship(plain).wait_recv()
+    add_parts([plain])
+    ship(passed).wait_recv()
+    add_parts([passed])
+    ship(joined).wait_recv()
+    add_parts([joined])
 
     def edges(pad, low, high, k):
         up = copy_to(pad.at[pl.ds(rows, HALO), :], low, hsend.at[k], hrecv.at[k], at(1))
@@ -195,7 +214,8 @@
         own[at_rows, :] = grad.T.astype(jnp.bfloat16)
         return carry
 
-    pieces = [(tile, rows - 2 * tile), (0, tile), (rows - tile, tile)]
+    half = tiles // 2 * tile
+    pieces = [(tile, half - tile), (half, rows - tile - half), (0, tile), (rows - tile, tile)]
 
     def grads(p, m):
         cut = pl.ds(pieces[p][0], pieces[p][1])
@@ -210,6 +230,13 @@
             src, near.at[2 * j + 1, cut, :], xsend.at[p, j], xrecv.at[p, j], partner
         )
 
+    def relay(p):
+        cut = pl.ds(pieces[p][0], pieces[p][1])
+        return copy_to(
+            near_cut(p, joined), near.at[2 * direct, cut, :],
+            gsend.at[p, direct], grecv.at[p, direct], across,
+        )
+
     def own_cut(p):
         return own.at[pl.ds(pieces[p][0], pieces[p][1]), :]
 
@@ -217,39 +244,49 @@
         return near.at[2 * m, pl.ds(pieces[p][0], pieces[p][1]), :]
 
     lax.fori_loop(1, tiles - 1, adjoint, 0)
-    order = (0, 4, 1, 3)
-    for m in order:
-        grads(0, m).start()
-    hand(0, 2, own_cut(0)).start()
+    for p in (0, 1):
+        grads(p, joined).start()
+        grads(p, passed).start()
+        hand(p, 2, own_cut(p)).start()
     for c in adj_edges:
         c.wait()
     wpad[0:HALO, :] = lo2[...]
     wpad[rows + HALO : rows + 2 * HALO, :] = hi2[...]
     lax.fori_loop(0, 2, lambda j, c: adjoint(j * (tiles - 1), c), 0)
-    for p in (1, 2):
-        for m in order:
-            grads(p, m).start()
+    for p in (2, 3):
+        grads(p, joined).start()
+        grads(p, passed).start()
         hand(p, 2, own_cut(p)).start()
     keep = pltpu.make_async_copy(own, near.at[2 * 2], local_sem.at[5])
     keep.start()
-    for m in (1, 3, far):
-        for p in range(3):
-            grads(p, m).wait_recv()
-            hand(p, m, near_cut(p, m)).start()
-    for p in range(3):
-        grads(p, alone).wait_recv()
+    for p in range(4):
+        grads(p, joined).wait_recv()
+        relay(p).start()
+        grads(p, joined).wait_send()
+        grads(p, plain).start()
+    for p in range(4):
+        grads(p, direct).wait_recv()
+        hand(p, direct, near_cut(p, direct)).start()
+    for p in range(4):
+        grads(p, plain).wait_recv()
+        hand(p, far, near_cut(p, far)).start()
+    for p in range(4):
+        grads(p, passed).wait_recv()
+        hand(p, passed, near_cut(p, passed)).start()
     keep.wait()
-    for p in range(3):
+    for p in range(4):
         for j in range(4):
             out = hand(p, j + 1 - core, own_cut(p))
             out.wait_send()
             out.wait_recv()
-        for m in order:
-            grads(p, m).wait_send()
+        grads(p, passed).wait_send()
+        grads(p, plain).wait_send()
+        relay(p).wait_send()
     for j in range(4):
         swap(j).wait_send()
-    for m in order:
+    for m in (plain, direct, joined):
         ship(m).wait_send()
+    add_on.wait_send()
 
 
 def adjoint_kernel(
@@ -345,6 +382,7 @@
             pltpu.VMEM((5, rows, channels), jnp.bfloat16),
             pltpu.VMEM((4, rows, channels), jnp.bfloat16),
             pltpu.VMEM((5, rows, channels), jnp.bfloat16),
+            pltpu.VMEM((rows, channels), jnp.bfloat16),
             f32(rows + 2 * HALO, channels),
             f32(rows + 2 * HALO, channels),
             f32(rows, channels),
@@ -361,10 +399,11 @@
             pltpu.SemaphoreType.DMA((5,)),
             pltpu.SemaphoreType.DMA((4,)),
             pltpu.SemaphoreType.DMA((4,)),
-            pltpu.SemaphoreType.DMA((3, 5)),
-            pltpu.SemaphoreType.DMA((3, 5)),
-            pltpu.SemaphoreType.DMA((3, 4)),
-            pltpu.SemaphoreType.DMA((3, 4)),
+            pltpu.SemaphoreType.DMA((4, 5)),
+            pltpu.SemaphoreType.DMA((4, 5)),
+            pltpu.SemaphoreType.DMA((4, 4)),
+            pltpu.SemaphoreType.DMA((4, 4)),
+            pltpu.SemaphoreType.DMA((2,)),
         ],
         compiler_params=params(collective_id=0, has_side_effects=True),
         name="exchange_and_step",

time: 122 us -> 111 us (0.910)
  Pallas kernels: 118 us -> 108 us
    pallas_call x1, Pallas kernels: 83.6 us -> 73.1 us  [shards(): pl.pallas_call(functools.partial(middle_kernel, devices, tile), out_shape...]
where the time goes in v3:
time: 111 us
  Pallas kernels  108 us (97%)
  other arithmetic  2.02 us (2%)
    pallas_call x1, Pallas kernels, shards(): pl.pallas_call(functools.partial(middle_kernel, devices, tile), out_shape...  73.1 us
    pallas_call x1, Pallas kernels, shards(): pl.pallas_call(functools.partial(forward_kernel, per), out_shape=jax.Shap...  17.5 us
    pallas_call x1, Pallas kernels, shards(): pl.pallas_call(functools.partial(adjoint_kernel, per), out_shape=(jax.Sha...  17.3 us

profile of v3, /device:TPU:0, one launch (start us, length us, event | category | flops | bytes accessed | tf_op | source)
XLA Modules:
  0.0 110.5 jit_solution(5810938490043927393)
XLA Ops:
  0.6 0.7 subtract_add_fusion
  1.3 1.3 %fusion.2.slot_ref = s32[256]{0:T(256)} fusion(s32[256]{0:T(256)S(1)} %bitcast.11, s32[8192]{0:T(1024)} %param.14, s32[]{:T(128)S(6)} %select_n.4), kind=kLoop, calls=%fused_computation.4 | loop fusion | flops 2048 | bytes 3076 | tf_op jit(solution)/shard_map/add | solution.py:344
  2.7 17.5 %remap_forward.1 = bf16[144,128,128]{2,1,0:T(8,128)(2,1)} custom-call(s32[256]{0:T(256)} %src_ref.3, s32[256]{0:T(256)} %fusion.2.slot_ref, bf16[32,128,128]{2,1,0:T(8,128)(2,1)} %bitcast.8, s32[32,128]{1,0:T(8,128)} %bitcast.9, bf16[256,128,128]{2,1,0:T(8,128)(2,1)} %w_ref.3), custom_call_target="tpu_custom_call" | custom-call | tf_op jit(solution)/shard_map/remap_forward/pallas_call | solution.py:348
  20.2 73.1 %exchange_and_step.1 = (bf16[9,2048,128]{2,1,0:T(8,128)(2,1)}, bf16[2048,128]{1,0:T(8,128)(2,1)}, bf16[2048,128]{1,0:T(8,128)(2,1)}) custom-call(bf16[9,2048,128]{2,1,0:T(8,128)(2,1)} %bitcast.6, bf16[2048,128]{1,0:T(8,128)(2,1)} %atm_ref.1, f32[2048,128]{1,0:T(8,128)} %kappa_ref.1, bf16[128,128]{1,0:T(8,128)(2,1)} %mix_ref.3, bf16[2048,128]{1,0:T(8,128)(2,1)} %cot_ref.1), custom_call_target="tpu_custom_call" | custom-call | tf_op jit(solution)/shard_map/exchange_and_step/pallas_call | solution.py:372
  93.3 17.3 %remap_adjoint.1 = (bf16[2048,128]{1,0:T(8,128)(2,1)}, bf16[2048,128]{1,0:T(8,128)(2,1)}, bf16[32,128,128]{2,1,0:T(8,128)(2,1)}) custom-call(s32[256]{0:T(256)} %src_ref.3, s32[256]{0:T(256)} %fusion.2.slot_ref, bf16[144,128,128]{2,1,0:T(8,128)(2,1)} %bitcast.7, s32[32,128]{1,0:T(8,128)} %bitcast.10, bf16[128,128]{1,0:T(8,128)(2,1)} %mix_ref.3, ...), custom_call_target="tpu_custom_call" | custom-call | tf_op jit(solution)/shard_map/remap_adjoint/pallas_call | solution.py:413

commit v4 on v3

--- a/solution.py
+++ b/solution.py
@@ -10,7 +10,7 @@
 WIN = 4
 SPAN = 2 * WIN + 1
 HALO = 8
-STEPS = 16
+CHUNKS = 4
 VMEM_BYTES = 56 * 1024 * 1024
 
 
@@ -21,39 +21,64 @@
     return jnp.where(eye, jnp.broadcast_to(row, (size, size)), 0).astype(jnp.bfloat16)
 
 
-def forward_kernel(per, src_ref, slot_ref, ocean_ref, mask_ref, w_ref, out_ref, acc, xm):
-    step = pl.program_id(0)
-    tile = w_ref.shape[1]
-
-    @pl.when(step == 0)
-    def _():
-        def clear(i, carry):
-            acc[i] = jnp.zeros(acc.shape[1:], acc.dtype)
-            return carry
-
-        lax.fori_loop(0, acc.shape[0], clear, 0)
-
-        def mask_tile(i, carry):
-            keep = jnp.where(mask_ref[pl.ds(i, 1), :] == 1, 1.0, 0.0)
-            xm[i] = jnp.dot(
-                diagonal(keep, tile), ocean_ref[i], preferred_element_type=jnp.float32
-            ).astype(jnp.bfloat16)
-            return carry
-
-        lax.fori_loop(0, xm.shape[0], mask_tile, 0, unroll=4)
-
-    for k in range(per):
-        e = step * per + k
-        product = jnp.dot(w_ref[k], xm[src_ref[e]], preferred_element_type=jnp.float32)
-        acc[slot_ref[e]] += product
-
-    @pl.when(step == pl.num_programs(0) - 1)
-    def _():
-        def narrow(i, carry):
-            out_ref[i] = acc[i].astype(out_ref.dtype)
-            return carry
-
-        lax.fori_loop(0, acc.shape[0], narrow, 0, unroll=4)
+def fetch_all(w_hbm, wbuf, sems):
+    per = w_hbm.shape[0] // CHUNKS
+
+    def fetch(c):
+        cut = pl.ds(c * per, per)
+        return pltpu.make_async_copy(w_hbm.at[cut], wbuf.at[cut], sems.at[c])
+
+    for c in range(CHUNKS):
+        fetch(c).start()
+    return fetch, per
+
+
+def clear_all(acc):
+    def clear(i, carry):
+        acc[i] = jnp.zeros(acc.shape[1:], acc.dtype)
+        return carry
+
+    lax.fori_loop(0, acc.shape[0], clear, 0, unroll=4)
+
+
+def forward_kernel(src_ref, slot_ref, ocean_ref, mask_ref, w_hbm, out_hbm, acc, xm, wbuf, obuf, sems, osems):
+    tile = w_hbm.shape[1]
+    fetch, per = fetch_all(w_hbm, wbuf, sems)
+    clear_all(acc)
+
+    def mask_tile(i, carry):
+        keep = jnp.where(mask_ref[pl.ds(i, 1), :] == 1, 1.0, 0.0)
+        xm[i] = jnp.dot(
+            diagonal(keep, tile), ocean_ref[i], preferred_element_type=jnp.float32
+        ).astype(jnp.bfloat16)
+        return carry
+
+    lax.fori_loop(0, xm.shape[0], mask_tile, 0, unroll=8)
+
+    def block(c, carry):
+        fetch(c).wait()
+        for k in range(per):
+            e = c * per + k
+            product = jnp.dot(wbuf[e], xm[src_ref[e]], preferred_element_type=jnp.float32)
+            acc[slot_ref[e]] += product
+        return carry
+
+    lax.fori_loop(0, CHUNKS, block, 0)
+    group = acc.shape[0] // SPAN
+
+    def put(o):
+        cut = pl.ds(o * group, group)
+        return pltpu.make_async_copy(obuf.at[cut], out_hbm.at[cut], osems.at[o])
+
+    def narrow(o, carry):
+        for t in range(group):
+            obuf[o * group + t] = acc[o * group + t].astype(obuf.dtype)
+        put(o).start()
+        return carry
+
+    lax.fori_loop(0, SPAN, narrow, 0)
+    for o in range(SPAN):
+        put(o).wait()
 
 
 def middle_kernel(
@@ -290,40 +315,42 @@
 
 
 def adjoint_kernel(
-    per, src_ref, slot_ref, near_ref, mask_ref, mix_ref, w_ref, hval_ref, grad_ref,
-    next_ref, grad_out_ref, ocean_ref, acc,
+    src_ref, slot_ref, near_hbm, mask_ref, mix_ref, w_hbm, hval_ref, grad_ref,
+    next_ref, grad_out_ref, ocean_ref, acc, near, wbuf, sems, nsem,
 ):
-    step = pl.program_id(0)
-
-    @pl.when(step == 0)
-    def _():
-        def clear(i, carry):
-            acc[i] = jnp.zeros(acc.shape[1:], acc.dtype)
-            return carry
-
-        lax.fori_loop(0, acc.shape[0], clear, 0)
-
-    next_ref[...] = jnp.dot(
-        hval_ref[...], mix_ref[...], preferred_element_type=jnp.float32
-    ).astype(jnp.bfloat16)
-    grad_out_ref[...] = grad_ref[...]
-    for k in range(per):
-        e = step * per + k
-        product = jnp.dot(near_ref[slot_ref[e]], w_ref[k], preferred_element_type=jnp.float32)
-        acc[src_ref[e]] += product
-
-    @pl.when(step == pl.num_programs(0) - 1)
-    def _():
-        def finish(i, carry):
-            total = jnp.where(mask_ref[pl.ds(i, 1), :] == 1, acc[i], 0.0)
-            ocean_ref[i] = total.T.astype(jnp.bfloat16)
-            return carry
-
-        lax.fori_loop(0, acc.shape[0], finish, 0, unroll=2)
-
-
-def whole(shape):
-    return pl.BlockSpec(shape, lambda i, *_: (0,) * len(shape))
+    tiles_in = pltpu.make_async_copy(near_hbm, near, nsem.at[0])
+    tiles_in.start()
+    fetch, per = fetch_all(w_hbm, wbuf, sems)
+    clear_all(acc)
+    tile = w_hbm.shape[1]
+
+    def mixed(i, carry):
+        at_rows = pl.ds(pl.multiple_of(i * tile, tile), tile)
+        next_ref[at_rows, :] = jnp.dot(
+            hval_ref[at_rows, :], mix_ref[...], preferred_element_type=jnp.float32
+        ).astype(jnp.bfloat16)
+        grad_out_ref[at_rows, :] = grad_ref[at_rows, :]
+        return carry
+
+    lax.fori_loop(0, hval_ref.shape[0] // tile, mixed, 0, unroll=4)
+    tiles_in.wait()
+
+    def block(c, carry):
+        fetch(c).wait()
+        for k in range(per):
+            e = c * per + k
+            product = jnp.dot(near[slot_ref[e]], wbuf[e], preferred_element_type=jnp.float32)
+            acc[src_ref[e]] += product
+        return carry
+
+    lax.fori_loop(0, CHUNKS, block, 0)
+
+    def finish(i, carry):
+        total = jnp.where(mask_ref[pl.ds(i, 1), :] == 1, acc[i], 0.0)
+        ocean_ref[i] = total.T.astype(jnp.bfloat16)
+        return carry
+
+    lax.fori_loop(0, acc.shape[0], finish, 0, unroll=4)
 
 
 def shards(
@@ -338,36 +365,32 @@
     rows = atm_state.shape[0]
     atm = rows // tile
     slots = SPAN * atm
-    per = entries // STEPS
     dest = lax.dynamic_slice_in_dim(dest_device.reshape(-1), me * entries, entries)
     target = lax.dynamic_slice_in_dim(target_tile, me * entries, entries)
     slot = lax.rem(dest - me + WIN + devices, devices) * atm + target
     mask = ocean_mask.reshape(ocn, tile)
     params = functools.partial(pltpu.CompilerParams, vmem_limit_bytes=VMEM_BYTES)
 
+    vmem = pl.BlockSpec(memory_space=pltpu.VMEM)
+    hbm = pl.BlockSpec(memory_space=pl.ANY)
+    smem = pl.BlockSpec(memory_space=pltpu.SMEM)
     part = pl.pallas_call(
-        functools.partial(forward_kernel, per),
+        forward_kernel,
         out_shape=jax.ShapeDtypeStruct((slots, tile, channels), jnp.bfloat16),
-        grid_spec=pltpu.PrefetchScalarGridSpec(
-            num_scalar_prefetch=2,
-            grid=(STEPS,),
-            in_specs=[
-                whole((ocn, tile, channels)),
-                whole((ocn, tile)),
-                pl.BlockSpec((per, tile, tile), lambda i, *_: (i, 0, 0)),
-            ],
-            out_specs=whole((slots, tile, channels)),
-            scratch_shapes=[
-                pltpu.VMEM((slots, tile, channels), jnp.float32),
-                pltpu.VMEM((ocn, tile, channels), jnp.bfloat16),
-            ],
-        ),
+        in_specs=[smem, smem, vmem, vmem, hbm],
+        out_specs=hbm,
+        scratch_shapes=[
+            pltpu.VMEM((slots, tile, channels), jnp.float32),
+            pltpu.VMEM((ocn, tile, channels), jnp.bfloat16),
+            pltpu.VMEM((entries, tile, tile), jnp.bfloat16),
+            pltpu.VMEM((slots, tile, channels), jnp.bfloat16),
+            pltpu.SemaphoreType.DMA((CHUNKS,)),
+            pltpu.SemaphoreType.DMA((SPAN,)),
+        ],
         compiler_params=params(),
         name="remap_forward",
     )(source_tile, slot, ocean_field.reshape(ocn, tile, channels), mask, remap_weight)
 
-    vmem = pl.BlockSpec(memory_space=pltpu.VMEM)
-    hbm = pl.BlockSpec(memory_space=pl.ANY)
     f32 = lambda *shape: pltpu.VMEM(shape, jnp.float32)
     near, grad, hval = pl.pallas_call(
         functools.partial(middle_kernel, devices, tile),
@@ -409,28 +432,22 @@
         name="exchange_and_step",
     )(part.reshape(SPAN, rows, channels), atm_state, kappa, mix, cotangent)
 
-    cut = pl.BlockSpec((rows // STEPS, channels), lambda i, *_: (i, 0))
     atm_next, atm_grad, ocean_grad = pl.pallas_call(
-        functools.partial(adjoint_kernel, per),
+        adjoint_kernel,
         out_shape=(
             jax.ShapeDtypeStruct((rows, channels), jnp.bfloat16),
             jax.ShapeDtypeStruct((rows, channels), jnp.bfloat16),
             jax.ShapeDtypeStruct((ocn, tile, channels), jnp.bfloat16),
         ),
-        grid_spec=pltpu.PrefetchScalarGridSpec(
-            num_scalar_prefetch=2,
-            grid=(STEPS,),
-            in_specs=[
-                whole((slots, tile, channels)),
-                whole((ocn, tile)),
-                whole((channels, channels)),
-                pl.BlockSpec((per, tile, tile), lambda i, *_: (i, 0, 0)),
-                cut,
-                cut,
-            ],
-            out_specs=(cut, cut, whole((ocn, tile, channels))),
-            scratch_shapes=[pltpu.VMEM((ocn, channels, tile), jnp.float32)],
-        ),
+        in_specs=[smem, smem, hbm, vmem, vmem, hbm, vmem, vmem],
+        out_specs=(vmem, vmem, vmem),
+        scratch_shapes=[
+            pltpu.VMEM((ocn, channels, tile), jnp.float32),
+            pltpu.VMEM((slots, tile, channels), jnp.bfloat16),
+            pltpu.VMEM((entries, tile, tile), jnp.bfloat16),
+            pltpu.SemaphoreType.DMA((CHUNKS,)),
+            pltpu.SemaphoreType.DMA((1,)),
+        ],
         compiler_params=params(),
         name="remap_adjoint",
     )(

time: 111 us -> 95.4 us (0.86)
  Pallas kernels: 108 us -> 92.5 us
    pallas_call x2, Pallas kernels: 34.8 us -> 19.4 us  [the longest x1 10.9 us: shards(): pl.pallas_call(adjoint_kernel, out_shape=(jax.ShapeDtypeStruct((rows, cha...]
where the time goes in v4:
time: 95.4 us; the launch traced here: 95.2 us
  Pallas kernels  92.5 us (97%)
  other arithmetic  2.02 us (2%)
    pallas_call x1, Pallas kernels, shards(): pl.pallas_call(functools.partial(middle_kernel, devices, tile), out_shape...  73.1 us
    pallas_call x1, Pallas kernels, shards(): pl.pallas_call(adjoint_kernel, out_shape=(jax.ShapeDtypeStruct((rows, cha...  10.9 us
    pallas_call x1, Pallas kernels, shards(): pl.pallas_call(forward_kernel, out_shape=jax.ShapeDtypeStruct((slots, til...  8.52 us
    add x2, other arithmetic, shards(): slot = lax.rem(dest - me + WIN + devices, devices) * atm + target  2.02 us

profile of v4, /device:TPU:0, one launch (start us, length us, event | category | flops | bytes accessed | tf_op | source)
XLA Modules:
  0.0 95.2 jit_solution(5980536924742657288)
XLA Ops:
  0.6 0.7 subtract_add_fusion
  1.3 1.3 %fusion.2.slot_ref = s32[256]{0:T(256)} fusion(s32[256]{0:T(256)S(1)} %bitcast.11, s32[8192]{0:T(1024)} %param.14, s32[]{:T(128)S(6)} %select_n.4), kind=kLoop, calls=%fused_computation.4 | loop fusion | flops 2048 | bytes 3076 | tf_op jit(solution)/shard_map/add | solution.py:370
  2.7 8.5 %remap_forward.1 = bf16[144,128,128]{2,1,0:T(8,128)(2,1)} custom-call(s32[256]{0:T(256)} %src_ref.3, s32[256]{0:T(256)} %fusion.2.slot_ref, bf16[32,128,128]{2,1,0:T(8,128)(2,1)} %bitcast.8, s32[32,128]{1,0:T(8,128)} %bitcast.9, bf16[256,128,128]{2,1,0:T(8,128)(2,1)} %w_hbm.3), custom_call_target="tpu_custom_call" | custom-call | tf_op jit(solution)/shard_map/remap_forward/pallas_call | solution.py:377
  11.2 73.1 %exchange_and_step.1 = (bf16[9,2048,128]{2,1,0:T(8,128)(2,1)}, bf16[2048,128]{1,0:T(8,128)(2,1)}, bf16[2048,128]{1,0:T(8,128)(2,1)}) custom-call(bf16[9,2048,128]{2,1,0:T(8,128)(2,1)} %bitcast.6, bf16[2048,128]{1,0:T(8,128)(2,1)} %atm_ref.1, f32[2048,128]{1,0:T(8,128)} %kappa_ref.1, bf16[128,128]{1,0:T(8,128)(2,1)} %mix_ref.3, bf16[2048,128]{1,0:T(8,128)(2,1)} %cot_ref.1), custom_call_target="tpu_custom_call" | custom-call | tf_op jit(solution)/shard_map/exchange_and_step/pallas_call | solution.py:395
  84.2 10.9 %remap_adjoint.1 = (bf16[2048,128]{1,0:T(8,128)(2,1)}, bf16[2048,128]{1,0:T(8,128)(2,1)}, bf16[32,128,128]{2,1,0:T(8,128)(2,1)}) custom-call(s32[256]{0:T(256)} %src_ref.3, s32[256]{0:T(256)} %fusion.2.slot_ref, bf16[144,128,128]{2,1,0:T(8,128)(2,1)} %bitcast.7, s32[32,128]{1,0:T(8,128)} %bitcast.10, bf16[128,128]{1,0:T(8,128)(2,1)} %mix_ref.3, ...), custom_call_target="tpu_custom_call" | custom-call | tf_op jit(solution)/shard_map/remap_adjoint/pallas_call | solution.py:435

commit v5 on v4

--- a/solution.py
+++ b/solution.py
@@ -149,7 +149,6 @@
     combine(far)
     ship(plain).start()
     combine(direct)
-    ship(direct).start()
     swap(1 + core).wait_recv()
 
     def adjoint_mix(i, carry):
@@ -179,6 +178,7 @@
         lax.fori_loop(0, tiles, body, 0, unroll=2)
 
     add_on.wait_recv()
+    ship(direct).start()
 
     def join(i, carry):
         at_rows = pl.ds(pl.multiple_of(i * tile, tile), tile)

time: 95.4 us -> 96.9 us (1.016); the launches traced: 95.2 us -> 95.1 us
  no operation moved by 1% of the time
where the time goes in v5:
time: 96.9 us; the launch traced here: 95.1 us
  Pallas kernels  92.4 us (95%)
  other arithmetic  2.02 us (2%)
    pallas_call x1, Pallas kernels, shards(): pl.pallas_call(functools.partial(middle_kernel, devices, tile), out_shape...  73 us
    pallas_call x1, Pallas kernels, shards(): pl.pallas_call(adjoint_kernel, out_shape=(jax.ShapeDtypeStruct((rows, cha...  10.9 us
    pallas_call x1, Pallas kernels, shards(): pl.pallas_call(forward_kernel, out_shape=jax.ShapeDtypeStruct((slots, til...  8.52 us
    add x2, other arithmetic, shards(): slot = lax.rem(dest - me + WIN + devices, devices) * atm + target  2.02 us

profile of v5, /device:TPU:0, one launch (start us, length us, event | category | flops | bytes accessed | tf_op | source)
XLA Modules:
  0.0 95.1 jit_solution(10307043156457845578)
XLA Ops:
  0.6 0.7 subtract_add_fusion
  1.3 1.3 %fusion.2.slot_ref = s32[256]{0:T(256)} fusion(s32[256]{0:T(256)S(1)} %bitcast.11, s32[8192]{0:T(1024)} %param.14, s32[]{:T(128)S(6)} %select_n.4), kind=kLoop, calls=%fused_computation.4 | loop fusion | flops 2048 | bytes 3076 | tf_op jit(solution)/shard_map/add | solution.py:370
  2.7 8.5 %remap_forward.1 = bf16[144,128,128]{2,1,0:T(8,128)(2,1)} custom-call(s32[256]{0:T(256)} %src_ref.3, s32[256]{0:T(256)} %fusion.2.slot_ref, bf16[32,128,128]{2,1,0:T(8,128)(2,1)} %bitcast.8, s32[32,128]{1,0:T(8,128)} %bitcast.9, bf16[256,128,128]{2,1,0:T(8,128)(2,1)} %w_hbm.3), custom_call_target="tpu_custom_call" | custom-call | tf_op jit(solution)/shard_map/remap_forward/pallas_call | solution.py:377
  11.2 73.0 %exchange_and_step.1 = (bf16[9,2048,128]{2,1,0:T(8,128)(2,1)}, bf16[2048,128]{1,0:T(8,128)(2,1)}, bf16[2048,128]{1,0:T(8,128)(2,1)}) custom-call(bf16[9,2048,128]{2,1,0:T(8,128)(2,1)} %bitcast.6, bf16[2048,128]{1,0:T(8,128)(2,1)} %atm_ref.1, f32[2048,128]{1,0:T(8,128)} %kappa_ref.1, bf16[128,128]{1,0:T(8,128)(2,1)} %mix_ref.3, bf16[2048,128]{1,0:T(8,128)(2,1)} %cot_ref.1), custom_call_target="tpu_custom_call" | custom-call | tf_op jit(solution)/shard_map/exchange_and_step/pallas_call | solution.py:395
  84.2 10.9 %remap_adjoint.1 = (bf16[2048,128]{1,0:T(8,128)(2,1)}, bf16[2048,128]{1,0:T(8,128)(2,1)}, bf16[32,128,128]{2,1,0:T(8,128)(2,1)}) custom-call(s32[256]{0:T(256)} %src_ref.3, s32[256]{0:T(256)} %fusion.2.slot_ref, bf16[144,128,128]{2,1,0:T(8,128)(2,1)} %bitcast.7, s32[32,128]{1,0:T(8,128)} %bitcast.10, bf16[128,128]{1,0:T(8,128)(2,1)} %mix_ref.3, ...), custom_call_target="tpu_custom_call" | custom-call | tf_op jit(solution)/shard_map/remap_adjoint/pallas_call | solution.py:435
